TPU v7x, 512 devices: a whole 4x4x16 slice. The times are simulated.
512 devices in a mesh: dp: 32 (over y, x, core), tensor: 16 (over z).
Axes of the slice: x: 4, y: 4, z: 16, core: 2. Of those that a mesh axis runs over, the one named last changes fastest.
Arguments:
- gradient: bfloat16 [32, 384, 28672], P('dp', None, 'tensor'), may hold values from -80 to 80
- error: bfloat16 [32, 384, 28672], P('dp', None, 'tensor'), may hold values from -3 to 3
- q_prev: bfloat16 [28672, 128], P('tensor'), may hold values from -6 to 6
Outputs:
- new_error: bfloat16 [32, 384, 28672], P('dp', None, 'tensor')
- q_next: bfloat16 [28672, 128], P('tensor')
All inputs are finite; a program needn't handle non-finite values.
Results may differ from a plain program's by a relative error of at most 0.013.
Values may be sent and summed in bfloat16 or wider, within the bound.
No kernel may reach another device: no remote copies, remote signals or barrier semaphores. Data moves between devices by JAX's collectives and lax.ppermute only.
A program may use at most 64 MiB of HBM per device.

v0:
```python
import jax
import jax.numpy as jnp
from jax import lax
from jax.sharding import PartitionSpec as P


def orthonormal(p_block, gram):
    lower = jnp.linalg.cholesky(gram)
    return lax.linalg.triangular_solve(
        lower, p_block, left_side=False, lower=True, transpose_a=True
    ).astype(jnp.bfloat16)


def on_device(gradient, error, q_prev):
    combined = (gradient[0].astype(jnp.float32) + error[0].astype(jnp.float32)).astype(jnp.bfloat16)
    replicas = lax.axis_size("dp")
    p_local = jnp.dot(combined, q_prev, preferred_element_type=jnp.float32)
    p_sum = lax.psum(p_local, ("dp", "tensor"))
    gram = jnp.dot(p_sum.T, p_sum, precision=lax.Precision.HIGHEST)
    basis = orthonormal(p_sum, gram)
    q_local = lax.dot_general(
        combined, basis, (((0,), (0,)), ((), ())), preferred_element_type=jnp.float32
    )
    q_total = lax.psum(q_local, "dp")
    q_next = (q_total / replicas).astype(jnp.bfloat16)
    decompressed = lax.dot_general(
        basis, q_next, (((1,), (1,)), ((), ())), preferred_element_type=jnp.float32
    )
    new_error = (combined.astype(jnp.float32) - decompressed).astype(jnp.bfloat16)
    return (new_error[None], q_next)


def solution(mesh):
    placed = (P("dp", None, "tensor"), P("dp", None, "tensor"), P("tensor", None))
    return jax.shard_map(
        on_device,
        mesh=mesh,
        in_specs=placed,
        out_specs=(P("dp", None, "tensor"), P("tensor", None)),
        check_vma=False,
    )
```

profile of v0, /device:TPU:1, one launch (start us, length us, event | category | flops | bytes accessed | tf_op | source)
XLA Modules:
  0.0 639.4 jit_solution(6430612603906594062)
XLA Ops:
  7.2 0.0 copy-start
  7.2 0.0 all-reduce.3.cloned.1.call-start
  7.2 1.0 copy-done
  8.2 0.0 copy-start.2
  8.2 3.1 fusion.8
  11.3 0.0 all-reduce.3.cloned.1.call-update
  11.3 0.0 all-reduce.5.cloned.1.call-start
  11.3 462.0 %all-reduce.3.cloned.1.call-done = f32[384,128]{1,0:T(8,128)} async-done(((f32[384,128]{1,0:T(8,128)}), f32[384,128]{1,0:T(8,128)}) %all-reduce.3.cloned.1.call-update) | async-done | bytes 196624 | tf_op jit(solution)/shard_map/psum | solution.py:18
  473.3 1.5 fusion.10
  474.9 0.1 copy.5
  475.0 11.7 %cholesky.16 = f32[128,128]{1,0:T(8,128)S(1)} custom-call(f32[128,128]{1,0:T(8,128)S(1)} %fusion.5), custom_call_target="Cholesky" | custom-call | tf_op jit(solution)/shard_map/jit(cholesky)/cholesky | solution.py:8
  486.7 0.6 compare_reduce_fusion
  487.4 0.7 fusion.3
  488.0 9.8 %custom-call.6 = f32[1,128,128]{1,2,0:T(8,128)S(1)} custom-call(f32[1,128,128]{2,1,0:T(8,128)S(1)} %fusion.3), custom_call_target="InvertDiagBlocksLowerTriangular" | custom-call | tf_op jit(solution)/shard_map/triangular_solve | solution.py:9
  497.8 1.2 convolution_convert_fusion
  499.1 0.0 copy-done.2
  499.1 0.0 copy-done.1
  499.1 1.5 fusion.6
  500.6 0.0 all-reduce.5.cloned.1.call-update
  500.6 129.1 %all-reduce.5.cloned.1.call-done = f32[1792,128]{1,0:T(8,128)} async-done(((f32[1792,128]{1,0:T(8,128)}), f32[1792,128]{1,0:T(8,128)}) %all-reduce.5.cloned.1.call-update) | async-done | bytes 917520 | tf_op jit(solution)/shard_map/psum | solution.py:24
  629.7 1.2 multiply_convert_fusion
  630.9 0.0 copy-start.3
  631.0 1.6 fusion.1
  632.6 0.0 copy-done.3
  (3 shorter events, 0.1 us)
Async XLA Ops:
  7.2 1.0 copy-start
  7.2 466.2 %all-reduce.3.cloned.1.call-start = ((), (), s32[]{:S(2)}) async-start(), calls=%async_computation | async-start | bytes 393216 | tf_op jit(solution)/shard_map/psum | solution.py:18
  8.2 490.9 %copy-start.2 = (bf16[1,384,1792]{2,1,0:T(8,128)(2,1)S(1)}, bf16[1,384,1792]{2,1,0:T(8,128)(2,1)}, u32[]{:S(2)}) copy-start(bf16[1,384,1792]{2,1,0:T(8,128)(2,1)} %param.3) | copy-start | bytes 4128772
  11.3 487.8 %copy-start.1 = (bf16[1,384,1792]{2,1,0:T(8,128)(2,1)S(1)}, bf16[1,384,1792]{2,1,0:T(8,128)(2,1)}, u32[]{:S(2)}) copy-start(bf16[1,384,1792]{2,1,0:T(8,128)(2,1)} %param.4) | copy-start | bytes 4128772
  11.3 618.4 %all-reduce.5.cloned.1.call-start = ((), (), s32[]{:S(2)}) async-start(), calls=%async_computation.1 | async-start | bytes 1835008 | tf_op jit(solution)/shard_map/psum | solution.py:24
  630.9 1.6 copy-start.3
Sparse Core Ops, SparseCore 0:
  14.0 459.2 all-reduce.2
  500.8 128.8 all-reduce.4
where the time goes:
time: 640 us; the launch traced here: 639 us
  waiting for transfers between devices  591 us (92%)
  other arithmetic  24.1 us (4%)
  between operations  14.1 us (2%)
  matrix products  8.94 us (1%)
    psum x1, waiting for transfers between devices, on_device(): p_sum = lax.psum(p_local, ('dp', 'tensor'))  462 us
    psum x1, waiting for transfers between devices, on_device(): q_total = lax.psum(q_local, 'dp')  129 us
  transfers between devices with their start and end apart: 2, of which 2 were waited for; matrix products, arithmetic and copies ran while one was open for 0% of the time, Pallas kernels for 0%

commit v1 on v0

--- a/solution.py
+++ b/solution.py
@@ -2,6 +2,14 @@
 import jax.numpy as jnp
 from jax import lax
 from jax.sharding import PartitionSpec as P
+
+
+def exchange(pieces, axis):
+    return lax.all_to_all(pieces, axis, 0, 0)
+
+
+def gather(piece, axis):
+    return exchange(jnp.broadcast_to(piece[None], (lax.axis_size(axis),) + piece.shape), axis)
 
 
 def orthonormal(p_block, gram):
@@ -12,16 +20,24 @@
 
 
 def on_device(gradient, error, q_prev):
+    rows, cols = gradient.shape[1:]
+    rank = q_prev.shape[1]
+    replicas = lax.axis_size("dp")
+    slabs = cols // rank
     combined = (gradient[0].astype(jnp.float32) + error[0].astype(jnp.float32)).astype(jnp.bfloat16)
-    replicas = lax.axis_size("dp")
     p_local = jnp.dot(combined, q_prev, preferred_element_type=jnp.float32)
-    p_sum = lax.psum(p_local, ("dp", "tensor"))
+    slabbed = combined.reshape(rows, slabs, rank).transpose(1, 0, 2).reshape(replicas, -1, rank)
+
+    p_pieces = exchange(jnp.pad(p_local, ((0, 128), (0, 0))).reshape(replicas, -1, rank), "dp")
+    p_piece = jnp.sum(gather(jnp.sum(p_pieces, axis=0), "tensor"), axis=0)
+    p_sum = gather(p_piece, "dp").reshape(-1, rank)[:rows]
+
+    total_piece = jnp.sum(exchange(slabbed, "dp").astype(jnp.float32), axis=0).astype(jnp.bfloat16)
+    total = gather(total_piece, "dp").reshape(slabs, rows, rank)
+
     gram = jnp.dot(p_sum.T, p_sum, precision=lax.Precision.HIGHEST)
     basis = orthonormal(p_sum, gram)
-    q_local = lax.dot_general(
-        combined, basis, (((0,), (0,)), ((), ())), preferred_element_type=jnp.float32
-    )
-    q_total = lax.psum(q_local, "dp")
+    q_total = jnp.einsum("src,rk->sck", total, basis, preferred_element_type=jnp.float32).reshape(cols, rank)
     q_next = (q_total / replicas).astype(jnp.bfloat16)
     decompressed = lax.dot_general(
         basis, q_next, (((1,), (1,)), ((), ())), preferred_element_type=jnp.float32

time: 640 us -> 127 us (0.20)
  waiting for transfers between devices: 591 us -> 38.5 us
  starting transfers between devices: 0.08 us -> 29.7 us
  blocking collectives: 0 us -> 18.5 us
  between operations: 14.1 us -> 0.81 us
    psum x2 -> x0, waiting for transfers between devices: 591 us -> none  [the longest x1 462 us: on_device(): p_sum = lax.psum(p_local, ('dp', 'tensor'))]
    all_to_all x0 -> x4, waiting for transfers between devices: none -> 38.5 us  [exchange(): return lax.all_to_all(pieces, axis, 0, 0)]
    all_to_all x0 -> x4, starting transfers between devices: none -> 29.7 us  [exchange(): return lax.all_to_all(pieces, axis, 0, 0)]
    all_to_all x0 -> x1, blocking collectives: none -> 18.5 us  [exchange(): return lax.all_to_all(pieces, axis, 0, 0)]
  transfers between devices with their start and end apart: 2 -> 4, of which waited for: 2 -> 3; matrix products, arithmetic and copies ran while one was open for 0% -> 22% of each run, Pallas kernels for 0% -> 0%
where the time goes in v1:
time: 127 us; the launch traced here: 126 us
  waiting for transfers between devices  38.5 us (30%)
  starting transfers between devices  29.7 us (23%)
  other arithmetic  25.4 us (20%)
  blocking collectives  18.5 us (15%)
  local copies, waits for them, and re-layouts  7.4 us (6%)
  matrix products  5.72 us (5%)
    all_to_all x4, waiting for transfers between devices, exchange(): return lax.all_to_all(pieces, axis, 0, 0)  38.5 us
    all_to_all x4, starting transfers between devices, exchange(): return lax.all_to_all(pieces, axis, 0, 0)  29.7 us
    all_to_all x1, blocking collectives, exchange(): return lax.all_to_all(pieces, axis, 0, 0)  18.5 us
    another operation x3, other arithmetic, orthonormal(): lower = jnp.linalg.cholesky(gram)  12.5 us
    another operation x2, other arithmetic, orthonormal(): lax.linalg.triangular_solve(lower, p_block, left_side=False, lower=True,...  10.5 us
    broadcast_in_dim x3, local copies, waits for them, and re-layouts, gather(): jnp.broadcast_to(piece[None], (lax.axis_size(axis),) + piece.shape)  2.64 us
  transfers between devices with their start and end apart: 4, of which 3 were waited for; matrix products, arithmetic and copies ran while one was open for 22% of the time, Pallas kernels for 0%

profile of v1, /device:TPU:1, one launch (start us, length us, event | category | flops | bytes accessed | tf_op | source)
XLA Modules:
  0.0 126.0 jit_solution(7362090641298537474)
XLA Ops:
  0.6 2.1 %add_convert_fusion = bf16[1,384,1792]{2,1,0:T(8,128)(2,1)S(1)} fusion(bf16[1,384,1792]{2,1,0:T(8,128)(2,1)} %param.4, bf16[1,384,1792]{2,1,0:T(8,128)(2,1)} %param.3), kind=kLoop, calls=%fused_computation.2 | loop fusion | flops 2752512 | bytes 4128768 | tf_op jit(solution)/shard_map/convert_element_type | solution.py:27
  2.8 0.5 fusion.3
  3.3 18.5 %all_to_all.25 = f32[32,16,128]{2,1,0:T(8,128)S(1)} all-to-all(f32[32,16,128]{2,1,0:T(8,128)S(1)} %bitcast.37), channel_id=1, replica_groups=mesh['dp'=32,'tensor'=16] {'dp'}, dimensions={0} | all-to-all | bytes 524288 | tf_op jit(solution)/shard_map/all_to_all | solution.py:8
  21.9 0.7 broadcast_in_dim.9
  22.6 13.7 %all-to-all-start.1 = ((f32[16,16,128]{2,1,0:T(8,128)}), f32[16,16,128]{2,1,0:T(8,128)S(1)}, u32[]{:S(2)}, u32[]{:S(2)}) async-start(f32[16,16,128]{2,1,0:T(8,128)} %broadcast_in_dim.9), calls=%async_computation.1 | async-start | bytes 262144 | tf_op jit(solution)/shard_map/all_to_all | solution.py:8
  36.3 0.9 copy.24
  37.1 1.6 %copy.25 = bf16[14,384,128]{2,1,0:T(8,128)(2,1)} copy(bf16[14,384,128]{1,2,0:T(8,128)(2,1)S(1)} %bitcast.36) | data formatting | bytes 2752512 | tf_op jit(solution)/shard_map/transpose | solution.py:29
  38.7 9.7 %all-to-all-done.1 = f32[16,16,128]{2,1,0:T(8,128)S(1)} async-done(((f32[16,16,128]{2,1,0:T(8,128)}), f32[16,16,128]{2,1,0:T(8,128)S(1)}, u32[]{:S(2)}, u32[]{:S(2)}) %all-to-all-start.1) | async-done | bytes 131104 | tf_op jit(solution)/shard_map/all_to_all | solution.py:8
  48.4 6.6 %all-to-all-start.3 = ((bf16[32,168,128]{2,1,0:T(8,128)(2,1)}), bf16[32,168,128]{2,1,0:T(8,128)(2,1)S(1)}, u32[]{:S(2)}, u32[]{:S(2)}) async-start(bf16[32,168,128]{2,1,0:T(8,128)(2,1)} %bitcast.34), calls=%async_computation.3 | async-start | bytes 2752512 | tf_op jit(solution)/shard_map/all_to_all | solution.py:8
  55.0 19.9 %all-to-all-done.3 = bf16[32,168,128]{2,1,0:T(8,128)(2,1)S(1)} async-done(((bf16[32,168,128]{2,1,0:T(8,128)(2,1)}), bf16[32,168,128]{2,1,0:T(8,128)(2,1)S(1)}, u32[]{:S(2)}, u32[]{:S(2)}) %all-to-all-start.3) | async-done | bytes 1376288 | tf_op jit(solution)/shard_map/all_to_all | solution.py:8
  75.0 0.7 broadcast_in_dim.10
  75.7 5.5 %all-to-all-start.2 = ((f32[32,16,128]{2,1,0:T(8,128)}), f32[32,16,128]{2,1,0:T(8,128)S(1)}, u32[]{:S(2)}, u32[]{:S(2)}) async-start(f32[32,16,128]{2,1,0:T(8,128)} %broadcast_in_dim.10), calls=%async_computation.2 | async-start | bytes 524288 | tf_op jit(solution)/shard_map/all_to_all | solution.py:8
  81.4 8.8 %all-to-all-done.2 = f32[32,16,128]{2,1,0:T(8,128)S(1)} async-done(((f32[32,16,128]{2,1,0:T(8,128)}), f32[32,16,128]{2,1,0:T(8,128)S(1)}, u32[]{:S(2)}, u32[]{:S(2)}) %all-to-all-start.2) | async-done | bytes 262176 | tf_op jit(solution)/shard_map/all_to_all | solution.py:8
  90.2 1.3 broadcast_in_dim.11
  91.5 3.9 %all-to-all-start.4 = ((bf16[32,168,128]{2,1,0:T(8,128)(2,1)}), bf16[32,168,128]{2,1,0:T(8,128)(2,1)S(1)}, u32[]{:S(2)}, u32[]{:S(2)}) async-start(bf16[32,168,128]{2,1,0:T(8,128)(2,1)} %broadcast_in_dim.11), calls=%async_computation.4 | async-start | bytes 2752512 | tf_op jit(solution)/shard_map/all_to_all | solution.py:8
  95.4 0.7 copy-done.2
  96.7 11.7 %cholesky.16 = f32[128,128]{1,0:T(8,128)S(1)} custom-call(f32[128,128]{1,0:T(8,128)S(1)} %fusion.8), custom_call_target="Cholesky" | custom-call | tf_op jit(solution)/shard_map/jit(cholesky)/cholesky | solution.py:16
  108.5 0.7 compare_reduce_fusion
  109.2 0.7 fusion.6
  109.9 9.8 %custom-call.6 = f32[1,128,128]{1,2,0:T(8,128)S(1)} custom-call(f32[1,128,128]{2,1,0:T(8,128)S(1)} %fusion.6), custom_call_target="InvertDiagBlocksLowerTriangular" | custom-call | tf_op jit(solution)/shard_map/triangular_solve | solution.py:17
  119.7 1.2 convolution_convert_fusion
  121.0 1.5 %copy.26 = bf16[14,128,384]{2,1,0:T(8,128)(2,1)} copy(bf16[14,128,384]{1,2,0:T(8,128)(2,1)S(1)} %bitcast.33) | data formatting | bytes 2752512 | tf_op jit(solution)/shard_map/src,rk->sck/dot_general | solution.py:40
  122.5 1.9 %fusion.2 = bf16[1792,128]{1,0:T(8,128)(2,1)S(1)} fusion(bf16[1792,384]{1,0:T(8,128)(2,1)} %bitcast.35, bf16[384,128]{1,0:T(8,128)(2,1)S(1)} %convolution_convert_fusion), kind=kOutput, calls=%fused_computation.5 | convolution fusion | flops 176619520 | bytes 1933312 | tf_op jit(solution)/shard_map/src,rk->sck/dot_general | solution.py:40
  124.4 1.6 %fusion.1 = bf16[1,384,1792]{2,1,0:T(8,128)(2,1)} fusion(bf16[384,128]{1,0:T(8,128)(2,1)S(1)} %convolution_convert_fusion, bf16[1792,128]{1,0:T(8,128)(2,1)S(1)} %fusion.2, bf16[1,384,1792]{2,1,0:T(8,128)(2,1)S(1)} %add_convert_fusion), kind=kOutput, calls=%fused_computation.3 | convolution fusion | flops 178225152 | bytes 3309568 | tf_op jit(solution)/shard_map/dot_general | solution.py:42
  (15 shorter events, 0.9 us)
Async XLA Ops:
  0.6 2.1 %copy-start = (bf16[1792,128]{1,0:T(8,128)(2,1)S(1)}, bf16[1792,128]{1,0:T(8,128)(2,1)}, u32[]{:S(2)}) copy-start(bf16[1792,128]{1,0:T(8,128)(2,1)} %param.5) | copy-start | bytes 1376260
  22.6 25.9 %all-to-all-start.1 = ((f32[16,16,128]{2,1,0:T(8,128)}), f32[16,16,128]{2,1,0:T(8,128)S(1)}, u32[]{:S(2)}, u32[]{:S(2)}) async-start(f32[16,16,128]{2,1,0:T(8,128)} %broadcast_in_dim.9), calls=%async_computation.1 | async-start | bytes 262144 | tf_op jit(solution)/shard_map/all_to_all | solution.py:8
  48.4 26.5 %all-to-all-start.3 = ((bf16[32,168,128]{2,1,0:T(8,128)(2,1)}), bf16[32,168,128]{2,1,0:T(8,128)(2,1)S(1)}, u32[]{:S(2)}, u32[]{:S(2)}) async-start(bf16[32,168,128]{2,1,0:T(8,128)(2,1)} %bitcast.34), calls=%async_computation.3 | async-start | bytes 2752512 | tf_op jit(solution)/shard_map/all_to_all | solution.py:8
  75.7 14.5 %all-to-all-start.2 = ((f32[32,16,128]{2,1,0:T(8,128)}), f32[32,16,128]{2,1,0:T(8,128)S(1)}, u32[]{:S(2)}, u32[]{:S(2)}) async-start(f32[32,16,128]{2,1,0:T(8,128)} %broadcast_in_dim.10), calls=%async_computation.2 | async-start | bytes 524288 | tf_op jit(solution)/shard_map/all_to_all | solution.py:8
  91.5 29.5 %all-to-all-start.4 = ((bf16[32,168,128]{2,1,0:T(8,128)(2,1)}), bf16[32,168,128]{2,1,0:T(8,128)(2,1)S(1)}, u32[]{:S(2)}, u32[]{:S(2)}) async-start(bf16[32,168,128]{2,1,0:T(8,128)(2,1)} %broadcast_in_dim.11), calls=%async_computation.4 | async-start | bytes 2752512 | tf_op jit(solution)/shard_map/all_to_all | solution.py:8
  95.4 0.7 copy-start.2
  124.4 1.6 %copy-start.1 = (bf16[1792,128]{1,0:T(8,128)(2,1)}, bf16[1792,128]{1,0:T(8,128)(2,1)S(1)}, u32[]{:S(2)}) copy-start(bf16[1792,128]{1,0:T(8,128)(2,1)S(1)} %fusion.2) | copy-start | bytes 1376260

commit v2 on v0

v2 whole, which is shorter than its diff:
```python
import jax
import jax.numpy as jnp
from jax import lax
from jax.experimental import pallas as pl
from jax.experimental.pallas import tpu as pltpu
from jax.sharding import PartitionSpec as P

F32, BF16 = jnp.float32, jnp.bfloat16
LANES = 128
CHIPS = 16
STEP = 16
VMEM_LIMIT = 48 * 1024 * 1024


def params():
    return pltpu.CompilerParams(vmem_limit_bytes=VMEM_LIMIT)


def split(x):
    high = x.astype(BF16)
    return high, (x - high.astype(F32)).astype(BF16)


def whole(shape):
    return pl.BlockSpec(shape, lambda *_: (0,) * len(shape))


def combine_kernel(core_ref, g_ref, e_ref, own_ref, other_ref):
    core = core_ref[0]
    half = g_ref.shape[0] // 2
    for slab in range(g_ref.shape[1] // LANES):
        columns = slice(slab * LANES, (slab + 1) * LANES)
        for which, out_ref in ((core, own_ref), (1 - core, other_ref)):
            rows = pl.ds(pl.multiple_of(which * half, half), half)
            total = g_ref[rows, columns].astype(F32) + e_ref[rows, columns].astype(F32)
            out_ref[slab * half : (slab + 1) * half, :] = total.astype(BF16)


def combine(core, gradient, error):
    rows, cols = gradient.shape
    steps = 2
    slabs = cols // LANES
    out = jax.ShapeDtypeStruct((slabs * rows // 2, LANES), BF16)
    block = pl.BlockSpec((rows, cols // steps), lambda i: (0, i))
    out_block = pl.BlockSpec((slabs // steps * rows // 2, LANES), lambda i: (i, 0))
    return pl.pallas_call(
        combine_kernel,
        grid=(steps,),
        out_shape=(out, out),
        in_specs=[pl.BlockSpec(memory_space=pltpu.SMEM), block, block],
        out_specs=(out_block, out_block),
        compiler_params=params(),
        name="combine",
    )(core, gradient, error)


def pack_kernel(own_ref, got_ref, q_ref, out_ref):
    half = own_ref.shape[0] // (q_ref.shape[0] // LANES)
    span = out_ref.shape[1] - 2 * STEP
    p = jnp.zeros((half, LANES), F32)
    for slab in range(q_ref.shape[0] // LANES):
        rows = slice(slab * half, (slab + 1) * half)
        q = q_ref[slab * LANES : (slab + 1) * LANES, :]
        both = jnp.concatenate([own_ref[rows, :], got_ref[rows, :]], axis=1)
        p += jnp.dot(both, jnp.concatenate([q, q], axis=0), preferred_element_type=F32)
    high, low = split(p)
    for piece in range(CHIPS):
        if (piece + 1) * STEP <= half:
            out_ref[piece, :STEP, :] = high[piece * STEP : (piece + 1) * STEP, :]
            out_ref[piece, STEP : 2 * STEP, :] = low[piece * STEP : (piece + 1) * STEP, :]
        else:
            out_ref[piece, : 2 * STEP, :] = jnp.zeros((2 * STEP, LANES), BF16)
        first = piece * span
        count = min(span, own_ref.shape[0] - first)
        total = own_ref[first : first + count, :].astype(F32) + got_ref[first : first + count, :].astype(F32)
        out_ref[piece, 2 * STEP : 2 * STEP + count, :] = total.astype(BF16)
        if count < span:
            out_ref[piece, 2 * STEP + count :, :] = jnp.zeros((span - count, LANES), BF16)


def pack(own, got, q_prev, span):
    return pl.pallas_call(
        pack_kernel,
        out_shape=jax.ShapeDtypeStruct((CHIPS, 2 * STEP + span, LANES), BF16),
        compiler_params=params(),
        name="pack",
    )(own, got, q_prev)


def left_piece_kernel(in_ref, out_ref):
    total = in_ref[0, :STEP, :].astype(F32) + in_ref[0, STEP:, :].astype(F32)
    for chip in range(1, CHIPS):
        total += in_ref[chip, :STEP, :].astype(F32) + in_ref[chip, STEP:, :].astype(F32)
    for copy in range(out_ref.shape[0]):
        out_ref[copy] = total


def left_piece(pieces, copies):
    return pl.pallas_call(
        left_piece_kernel,
        grid=(1,),
        out_shape=jax.ShapeDtypeStruct((copies, STEP, LANES), F32),
        in_specs=[whole((CHIPS, 2 * STEP, LANES))],
        out_specs=whole((copies, STEP, LANES)),
        compiler_params=params(),
        name="left_piece",
    )(pieces)


def total_piece_kernel(in_ref, out_ref):
    total = in_ref[0, 2 * STEP :, :].astype(F32)
    for chip in range(1, CHIPS):
        total += in_ref[chip, 2 * STEP :, :].astype(F32)
    out_ref[...] = total.astype(BF16)


def total_piece(pieces):
    return pl.pallas_call(
        total_piece_kernel,
        out_shape=jax.ShapeDtypeStruct((pieces.shape[1] - 2 * STEP, LANES), BF16),
        compiler_params=params(),
        name="total_piece",
    )(pieces)


def repack_kernel(left_ref, total_ref, out_ref):
    p = left_ref[0]
    for at in range(1, left_ref.shape[0]):
        p += left_ref[at]
    high, low = split(p)
    total = total_ref[...]
    for chip in range(CHIPS):
        out_ref[chip, :STEP, :] = high
        out_ref[chip, STEP : 2 * STEP, :] = low
        out_ref[chip, 2 * STEP :, :] = total


def repack(left, total):
    return pl.pallas_call(
        repack_kernel,
        out_shape=jax.ShapeDtypeStruct((CHIPS, 2 * STEP + total.shape[0], LANES), BF16),
        compiler_params=params(),
        name="repack",
    )(left, total)


def left_half_kernel(in_ref, out_ref):
    for piece in range(out_ref.shape[0] // STEP):
        out_ref[piece * STEP : (piece + 1) * STEP, :] = in_ref[piece, :STEP, :].astype(F32) + in_ref[
            piece, STEP:, :
        ].astype(F32)


def left_half(pieces, half):
    return pl.pallas_call(
        left_half_kernel,
        grid=(1,),
        out_shape=jax.ShapeDtypeStruct((half, LANES), F32),
        in_specs=[whole((CHIPS, 2 * STEP, LANES))],
        out_specs=whole((half, LANES)),
        compiler_params=params(),
        name="left_half",
    )(pieces)


def spread(x, row=None, lane=None):
    if row is not None:
        x = x[row : row + 1, :]
    if lane is not None:
        x = x[:, lane : lane + 1]
    return jnp.broadcast_to(x, (8, LANES))


def inverse_factor(gram):
    groups = LANES // 8
    a = [gram[8 * g : 8 * g + 8, :] for g in range(groups)]
    row_of = lax.broadcasted_iota(jnp.int32, (8, LANES), 0)
    lane_of = lax.broadcasted_iota(jnp.int32, (8, LANES), 1)
    inv = [jnp.where(lane_of == row_of + 8 * g, 1.0, 0.0).astype(F32) for g in range(groups)]
    width = 4
    for first in range(0, LANES, width):
        g, s = first // 8, first % 8
        column = {h: [spread(a[h], lane=first + i) for i in range(width)] for h in range(g, groups)}
        d = [[spread(column[g][i], row=s + m) for i in range(m + 1)] for m in range(width)]
        low = [[None] * width for _ in range(width)]
        root = [None] * width
        for i in range(width):
            pivot = d[i][i]
            for k in range(i):
                pivot = pivot - low[i][k] * low[i][k]
            root[i] = lax.rsqrt(pivot)
            for m in range(i + 1, width):
                value = d[m][i]
                for k in range(i):
                    value = value - low[m][k] * low[i][k]
                low[m][i] = value * root[i]

        def solve(rows):
            y = []
            for m in range(width):
                value = rows[m]
                for k in range(m):
                    value = value - low[m][k] * y[k]
                y.append(value * root[m])
            z = [None] * width
            for m in reversed(range(width)):
                value = y[m]
                for k in range(m + 1, width):
                    value = value - low[k][m] * z[k]
                z[m] = value * root[m]
            return y, z

        _, za = solve([spread(a[g], row=s + m) for m in range(width)])
        yi, zi = solve([spread(inv[g], row=s + m) for m in range(width)])
        for h in range(g, groups):
            if h > g or s + width < 8:
                new_a, new_inv = a[h], inv[h]
                for i in range(width):
                    new_a = new_a - column[h][i] * za[i]
                    new_inv = new_inv - column[h][i] * zi[i]
                a[h] = new_a
                if h > g:
                    inv[h] = new_inv
                else:
                    inv[h] = jnp.where(row_of >= s + width, new_inv, inv[h])
        for m in range(width):
            inv[g] = jnp.where(row_of == s + m, yi[m], inv[g])
    return jnp.concatenate(inv, axis=0)


def basis_kernel(own_ref, other_ref, out_ref):
    def gram_of(p):
        return lax.dot_general(
            p, p, (((0,), (0,)), ((), ())), precision=lax.Precision.HIGHEST, preferred_element_type=F32
        )

    own, other = own_ref[...], other_ref[...]
    inverse = inverse_factor(gram_of(own) + gram_of(other))
    for at, p in enumerate((own, other)):
        out_ref[at] = lax.dot_general(
            p, inverse, (((1,), (1,)), ((), ())), precision=lax.Precision.HIGHEST, preferred_element_type=F32
        ).astype(BF16)


def bases(own, other):
    return pl.pallas_call(
        basis_kernel,
        out_shape=jax.ShapeDtypeStruct((2,) + own.shape, BF16),
        compiler_params=params(),
        cost_estimate=pl.CostEstimate(flops=20_000_000, bytes_accessed=15_000_000, transcendentals=0),
        name="basis",
    )(own, other)


def finish_kernel(replicas, core_ref, own_ref, other_ref, own_sum_ref, other_sum_ref, basis_ref, error_ref, q_ref):
    core = core_ref[0]
    half = basis_ref.shape[1]
    span = own_sum_ref.shape[1] - 2 * STEP

    def slab_of(ref, slab):
        at, end, parts = slab * half, (slab + 1) * half, []
        while at < end:
            piece = at // span
            stop = min(end, (piece + 1) * span)
            parts.append(ref[piece, 2 * STEP + at - piece * span : 2 * STEP + stop - piece * span, :])
            at = stop
        return jnp.concatenate(parts, axis=0)

    def pair_of(read, pair):
        return jnp.concatenate([read(2 * pair), read(2 * pair + 1)], axis=1)

    basis = (basis_ref[0], basis_ref[1])
    flipped = [b.astype(F32).T.astype(BF16) for b in basis]
    for pair in range(q_ref.shape[0] // (2 * LANES)):
        columns = slice(2 * pair * LANES, 2 * (pair + 1) * LANES)
        terms = [
            jnp.dot(flat, pair_of(lambda slab: slab_of(ref, slab), pair), preferred_element_type=F32)
            for flat, ref in zip(flipped, (own_sum_ref, other_sum_ref))
        ]
        scaled = (terms[0] + terms[1]) * (1.0 / replicas)
        q_ref[columns, :] = scaled.T.astype(BF16)
        right = scaled.astype(BF16)
        for which, ref, b in ((core, own_ref, basis[0]), (1 - core, other_ref, basis[1])):
            mine = pair_of(lambda slab: ref[slab * half : (slab + 1) * half, :], pair).astype(F32)
            rows = pl.ds(pl.multiple_of(which * half, half), half)
            error_ref[rows, columns] = (mine - jnp.dot(b, right, preferred_element_type=F32)).astype(BF16)


def finish(core, own, other, own_sum, other_sum, basis, replicas):
    rows, cols = 2 * basis.shape[1], own.shape[0] // basis.shape[1] * LANES
    vmem = pl.BlockSpec(memory_space=pltpu.VMEM)
    return pl.pallas_call(
        lambda *refs: finish_kernel(replicas, *refs),
        out_shape=(jax.ShapeDtypeStruct((rows, cols), BF16), jax.ShapeDtypeStruct((cols, LANES), BF16)),
        in_specs=[pl.BlockSpec(memory_space=pltpu.SMEM)] + [vmem] * 5,
        out_specs=(vmem, vmem),
        compiler_params=params(),
        name="finish",
    )(core, own, other, own_sum, other_sum, basis)


def on_device(gradient, error, q_prev):
    rows, cols = gradient.shape[1:]
    replicas = lax.axis_size("dp")
    half = rows // 2
    slab_rows = cols // LANES * half
    span = -(-slab_rows // CHIPS // 16) * 16
    core = (lax.axis_index("dp") % 2).astype(jnp.int32).reshape(1)
    twin = [(i, i ^ 1) for i in range(replicas)]
    same_core = [[2 * chip + c for chip in range(CHIPS)] for c in range(2)]

    def across_chips(pieces):
        return lax.all_to_all(pieces, "dp", 0, 0, axis_index_groups=same_core)

    own, other = combine(core, gradient[0], error[0])
    got = lax.ppermute(other, "dp", twin)
    pieces = across_chips(pack(own, got, q_prev, span))
    left = lax.all_to_all(left_piece(pieces, lax.axis_size("tensor")), "tensor", 0, 0)
    gathered = across_chips(repack(left, total_piece(pieces)))
    left_own = left_half(gathered, half)
    left_other = lax.ppermute(left_own, "dp", twin)
    gathered_other = lax.ppermute(gathered, "dp", twin)
    basis = bases(left_own, left_other)
    new_error, q_next = finish(core, own, other, gathered, gathered_other, basis, replicas)
    return (new_error[None], q_next)


def solution(mesh):
    placed = (P("dp", None, "tensor"), P("dp", None, "tensor"), P("tensor", None))
    return jax.shard_map(
        on_device,
        mesh=mesh,
        in_specs=placed,
        out_specs=(P("dp", None, "tensor"), P("tensor", None)),
        check_vma=False,
    )
```

time: 640 us -> 93.9 us (0.15)
  waiting for transfers between devices: 591 us -> 14.9 us
  blocking collectives: 0 us -> 31.7 us
  starting transfers between devices: 0.08 us -> 30.7 us
  other arithmetic: 24.1 us -> 0 us
  between operations: 14.1 us -> 0.73 us
  Pallas kernels: 0 us -> 12.8 us
  matrix products: 8.94 us -> 0 us
    psum x2 -> x0, waiting for transfers between devices: 591 us -> none  [the longest x1 462 us: on_device(): p_sum = lax.psum(p_local, ('dp', 'tensor'))]
    all_to_all x0 -> x2, blocking collectives: none -> 31.7 us  [across_chips(): return lax.all_to_all(pieces, 'dp', 0, 0, axis_index_groups=same_core)]
    another operation x5 -> x0, other arithmetic: 22.9 us -> none  [the longest x3 12.4 us: orthonormal(): lower = jnp.linalg.cholesky(gram)]
    ppermute x0 -> x3, starting transfers between devices: none -> 17.2 us  [the longest x1 8.79 us: on_device(): got = lax.ppermute(other, 'dp', twin)]
    all_to_all x0 -> x1, starting transfers between devices: none -> 13.4 us  [on_device(): lax.all_to_all(left_piece(pieces, lax.axis_size('tensor')), 'tensor', 0, 0)]
    pallas_call x0 -> x8, Pallas kernels: none -> 12.8 us  [the longest x1 7.73 us: bases(): pl.pallas_call(basis_kernel, out_shape=jax.ShapeDtypeStruct((2,) + own.sh...]
    all_to_all x0 -> x1, waiting for transfers between devices: none -> 11.9 us  [on_device(): lax.all_to_all(left_piece(pieces, lax.axis_size('tensor')), 'tensor', 0, 0)]
    dot_general x4 -> x0, matrix products: 7.7 us -> none  [the longest x1 3.08 us: on_device(): p_local = jnp.dot(combined, q_prev, preferred_element_type=jnp.float32)]
  transfers between devices with their start and end apart: 2 -> 4, of which waited for: 2 -> 3; matrix products, arithmetic and copies ran while one was open for 0% -> 0% of each run, Pallas kernels for 0% -> 8%
where the time goes in v2:
time: 93.9 us; the launch traced here: 93.5 us
  blocking collectives  31.7 us (34%)
  starting transfers between devices  30.7 us (33%)
  waiting for transfers between devices  14.9 us (16%)
  Pallas kernels  12.8 us (14%)
  local copies, waits for them, and re-layouts  2.67 us (3%)
    all_to_all x2, blocking collectives, across_chips(): return lax.all_to_all(pieces, 'dp', 0, 0, axis_index_groups=same_core)  31.7 us
    all_to_all x1, starting transfers between devices, on_device(): lax.all_to_all(left_piece(pieces, lax.axis_size('tensor')), 'tensor', 0, 0)  13.4 us
    all_to_all x1, waiting for transfers between devices, on_device(): lax.all_to_all(left_piece(pieces, lax.axis_size('tensor')), 'tensor', 0, 0)  11.9 us
    ppermute x1, starting transfers between devices, on_device(): got = lax.ppermute(other, 'dp', twin)  8.79 us
    pallas_call x1, Pallas kernels, bases(): pl.pallas_call(basis_kernel, out_shape=jax.ShapeDtypeStruct((2,) + own.sh...  7.73 us
    ppermute x1, starting transfers between devices, on_device(): gathered_other = lax.ppermute(gathered, 'dp', twin)  6.53 us
    pallas_call x1, Pallas kernels, finish(): pl.pallas_call(lambda *refs: finish_kernel(replicas, *refs), out_shape=(j...  2.96 us
    unnamed x6, local copies, waits for them, and re-layouts  2.67 us
  transfers between devices with their start and end apart: 4, of which 3 were waited for; matrix products, arithmetic and copies ran while one was open for 0% of the time, Pallas kernels for 8%

profile of v2, /device:TPU:1, one launch (start us, length us, event | category | flops | bytes accessed | tf_op | source)
XLA Modules:
  0.0 93.5 jit_solution(18058675374293462999)
XLA Ops:
  0.6 0.0 copy-start
  0.7 1.3 %copy-done = bf16[1,384,1792]{2,1,0:T(8,128)(2,1)S(1)} copy-done((bf16[1,384,1792]{2,1,0:T(8,128)(2,1)S(1)}, bf16[1,384,1792]{2,1,0:T(8,128)(2,1)}, u32[]{:S(2)}) %copy-start) | copy-done | bytes 1376280
  2.0 0.0 copy-start.1
  2.0 1.3 %copy-done.1 = bf16[1,384,1792]{2,1,0:T(8,128)(2,1)S(1)} copy-done((bf16[1,384,1792]{2,1,0:T(8,128)(2,1)S(1)}, bf16[1,384,1792]{2,1,0:T(8,128)(2,1)}, u32[]{:S(2)}) %copy-start.1) | copy-done | bytes 1376280
  3.3 0.0 copy-start.2
  3.3 0.6 combine.1
  3.9 8.8 %collective-permute-start = (bf16[2688,128]{1,0:T(8,128)(2,1)S(1)}, bf16[2688,128]{1,0:T(8,128)(2,1)S(1)}, u32[]{:S(2)}, u32[]{:S(2)}) collective-permute-start(bf16[2688,128]{1,0:T(8,128)(2,1)S(1)} %get-tuple-element.7.refs_2_), channel_id=1, source_target_pairs={{0,16},{16,0},{32,48},{48,32},{64,80},{80,64},{96,112},{112,96},{1... | collective-permute-start | bytes 2064392 | tf_op jit(solution)/shard_map/ppermute | solution.py:316
  12.7 1.7 %collective-permute-done.got_ref = bf16[2688,128]{1,0:T(8,128)(2,1)S(1)} collective-permute-done((bf16[2688,128]{1,0:T(8,128)(2,1)S(1)}, bf16[2688,128]{1,0:T(8,128)(2,1)S(1)}, u32[]{:S(2)}, u32[]{:S(2)}) %collective-permute-start) | collective-permute-done | bytes 688160 | tf_op jit(solution)/shard_map/ppermute | solution.py:316
  14.5 0.0 copy-done.2
  14.5 0.6 pack.1
  15.1 17.2 %all_to_all.15.in_ref = bf16[16,208,128]{2,1,0:T(8,128)(2,1)S(1)} all-to-all(bf16[16,208,128]{2,1,0:T(8,128)(2,1)S(1)} %pack.1), channel_id=1, replica_groups={{0,32,64,96,128,160,192,224,256,288,320,352,384,416,448,480},{16,48,80,..., dimensions={0} | all-to-all | bytes 1703936 | tf_op jit(solution)/shard_map/all_to_all | solution.py:313
  32.3 0.7 left_piece.1
  33.0 13.4 %all-to-all-start.1 = ((f32[16,16,128]{2,1,0:T(8,128)}), f32[16,16,128]{2,1,0:T(8,128)S(1)}, u32[]{:S(2)}, u32[]{:S(2)}) async-start(f32[16,16,128]{2,1,0:T(8,128)} %left_piece.1), calls=%async_computation.1 | async-start | bytes 262144 | tf_op jit(solution)/shard_map/all_to_all | solution.py:318
  46.4 0.1 total_piece.1.total_ref
  46.5 11.9 %all-to-all-done.1.left_ref = f32[16,16,128]{2,1,0:T(8,128)S(1)} async-done(((f32[16,16,128]{2,1,0:T(8,128)}), f32[16,16,128]{2,1,0:T(8,128)S(1)}, u32[]{:S(2)}, u32[]{:S(2)}) %all-to-all-start.1) | async-done | bytes 131104 | tf_op jit(solution)/shard_map/all_to_all | solution.py:318
  58.4 0.1 repack.1
  58.5 14.5 %all_to_all.16.in_ref.refs_3_ = bf16[16,208,128]{2,1,0:T(8,128)(2,1)S(1)} all-to-all(bf16[16,208,128]{2,1,0:T(8,128)(2,1)S(1)} %repack.1), channel_id=1, replica_groups={{0,32,64,96,128,160,192,224,256,288,320,352,384,416,448,480},{16,48,80,..., dimensions={0} | all-to-all | bytes 1703936 | tf_op jit(solution)/shard_map/all_to_all | solution.py:313
  73.1 6.5 %collective-permute-start.1 = (bf16[16,208,128]{2,1,0:T(8,128)(2,1)S(1)}, bf16[16,208,128]{2,1,0:T(8,128)(2,1)S(1)}, u32[]{:S(2)}, u32[]{:S(2)}) collective-permute-start(bf16[16,208,128]{2,1,0:T(8,128)(2,1)S(1)} %all_to_all.16.in_ref.refs_3_), channel_id=1, source_target_pairs={{0,16},{16,0},{32,48},{48,32},{64,80},{80,64},{96,112},{112,96},{1... | collective-permute-start | bytes 2555912 | tf_op jit(solution)/shard_map/ppermute | solution.py:322
  79.6 1.9 %collective-permute-start.2 = (f32[192,128]{1,0:T(8,128)S(1)}, f32[192,128]{1,0:T(8,128)S(1)}, u32[]{:S(2)}, u32[]{:S(2)}) collective-permute-start(f32[192,128]{1,0:T(8,128)S(1)} %left_half.1.own_ref), channel_id=1, source_target_pairs={{0,16},{16,0},{32,48},{48,32},{64,80},{80,64},{96,112},{112,96},{1... | collective-permute-start | bytes 294920 | tf_op jit(solution)/shard_map/ppermute | solution.py:321
  81.5 1.3 %collective-permute-done.2.other_ref = f32[192,128]{1,0:T(8,128)S(1)} collective-permute-done((f32[192,128]{1,0:T(8,128)S(1)}, f32[192,128]{1,0:T(8,128)S(1)}, u32[]{:S(2)}, u32[]{:S(2)}) %collective-permute-start.2) | collective-permute-done | bytes 98336 | tf_op jit(solution)/shard_map/ppermute | solution.py:321
  82.8 7.7 %basis.1.refs_5_ = bf16[2,192,128]{2,1,0:T(8,128)(2,1)S(1)} custom-call(f32[192,128]{1,0:T(8,128)S(1)} %left_half.1.own_ref, f32[192,128]{1,0:T(8,128)S(1)} %collective-permute-done.2.other_ref), custom_call_target="tpu_custom_call" | custom-call | flops 20000000 | bytes 15000000 | tf_op jit(solution)/shard_map/basis/pallas_call | solution.py:246
  90.5 0.0 collective-permute-done.1.refs_4_
  90.6 3.0 %finish.1 = (bf16[384,1792]{1,0:T(8,128)(2,1)}, bf16[1792,128]{1,0:T(8,128)(2,1)}) custom-call(s32[1]{0:T(128)} %bitcast.core_ref.refs_0_, bf16[2688,128]{1,0:T(8,128)(2,1)S(1)} %get-tuple-element.6.own_ref.refs_1_, bf16[2688,128]{1,0:T(8,128)(2,1)S(1)} %get-tuple-element.7.refs_2_, bf16[16,208,128]{2,1,0:T(8,128)(2,1)S(1)} %all_to_all.16.in_ref.refs_3_, ...), custom_call_target="tpu_custom_call" | custom-call | tf_op jit(solution)/shard_map/finish/pallas_call | solution.py:292
  (1 shorter events, 0.0 us)
Async XLA Ops:
  0.6 1.3 %copy-start = (bf16[1,384,1792]{2,1,0:T(8,128)(2,1)S(1)}, bf16[1,384,1792]{2,1,0:T(8,128)(2,1)}, u32[]{:S(2)}) copy-start(bf16[1,384,1792]{2,1,0:T(8,128)(2,1)} %param.3) | copy-start | bytes 4128772
  2.0 1.3 %copy-start.1 = (bf16[1,384,1792]{2,1,0:T(8,128)(2,1)S(1)}, bf16[1,384,1792]{2,1,0:T(8,128)(2,1)}, u32[]{:S(2)}) copy-start(bf16[1,384,1792]{2,1,0:T(8,128)(2,1)} %param.4) | copy-start | bytes 4128772
  3.3 11.2 %copy-start.2 = (bf16[1792,128]{1,0:T(8,128)(2,1)S(1)}, bf16[1792,128]{1,0:T(8,128)(2,1)}, u32[]{:S(2)}) copy-start(bf16[1792,128]{1,0:T(8,128)(2,1)} %q_ref.1) | copy-start | bytes 1376260
  3.9 10.5 %collective-permute-start = (bf16[2688,128]{1,0:T(8,128)(2,1)S(1)}, bf16[2688,128]{1,0:T(8,128)(2,1)S(1)}, u32[]{:S(2)}, u32[]{:S(2)}) collective-permute-start(bf16[2688,128]{1,0:T(8,128)(2,1)S(1)} %get-tuple-element.7.refs_2_), channel_id=1, source_target_pairs={{0,16},{16,0},{32,48},{48,32},{64,80},{80,64},{96,112},{112,96},{1... | collective-permute-start | bytes 2064392 | tf_op jit(solution)/shard_map/ppermute | solution.py:316
  33.0 25.5 %all-to-all-start.1 = ((f32[16,16,128]{2,1,0:T(8,128)}), f32[16,16,128]{2,1,0:T(8,128)S(1)}, u32[]{:S(2)}, u32[]{:S(2)}) async-start(f32[16,16,128]{2,1,0:T(8,128)} %left_piece.1), calls=%async_computation.1 | async-start | bytes 262144 | tf_op jit(solution)/shard_map/all_to_all | solution.py:318
  73.1 17.5 %collective-permute-start.1 = (bf16[16,208,128]{2,1,0:T(8,128)(2,1)S(1)}, bf16[16,208,128]{2,1,0:T(8,128)(2,1)S(1)}, u32[]{:S(2)}, u32[]{:S(2)}) collective-permute-start(bf16[16,208,128]{2,1,0:T(8,128)(2,1)S(1)} %all_to_all.16.in_ref.refs_3_), channel_id=1, source_target_pairs={{0,16},{16,0},{32,48},{48,32},{64,80},{80,64},{96,112},{112,96},{1... | collective-permute-start | bytes 2555912 | tf_op jit(solution)/shard_map/ppermute | solution.py:322
  79.6 3.2 %collective-permute-start.2 = (f32[192,128]{1,0:T(8,128)S(1)}, f32[192,128]{1,0:T(8,128)S(1)}, u32[]{:S(2)}, u32[]{:S(2)}) collective-permute-start(f32[192,128]{1,0:T(8,128)S(1)} %left_half.1.own_ref), channel_id=1, source_target_pairs={{0,16},{16,0},{32,48},{48,32},{64,80},{80,64},{96,112},{112,96},{1... | collective-permute-start | bytes 294920 | tf_op jit(solution)/shard_map/ppermute | solution.py:321

commit v3 on v0

v3 whole, which is shorter than its diff:
```python
import jax
import jax.numpy as jnp
from jax import lax
from jax.experimental import pallas as pl
from jax.experimental.pallas import tpu as pltpu
from jax.sharding import PartitionSpec as P

F32, BF16 = jnp.float32, jnp.bfloat16
LANES = 128
CHIPS = 16
STEP = 16
VMEM_LIMIT = 48 * 1024 * 1024
SENT_LIMIT = 52 * 1024 * 1024
KEPT_LIMIT = 52 * 1024 * 1024


def params():
    return pltpu.CompilerParams(vmem_limit_bytes=VMEM_LIMIT)


def split(x):
    high = x.astype(BF16)
    return high, (x - high.astype(F32)).astype(BF16)


def combined_half(which, g_in, e_in, out_ref, g_ref, e_ref, sems):
    half, cols = g_ref.shape
    chunks = sems.shape[1]
    count = half // chunks
    copies = []
    for chunk in range(chunks):
        rows = pl.ds(pl.multiple_of(which * half + chunk * count, 16), count)
        here = slice(chunk * count, (chunk + 1) * count)
        pair = [
            pltpu.make_async_copy(g_in.at[rows, :], g_ref.at[here, :], sems.at[0, chunk]),
            pltpu.make_async_copy(e_in.at[rows, :], e_ref.at[here, :], sems.at[1, chunk]),
        ]
        for copy in pair:
            copy.start()
        copies.append(pair)
    for chunk in range(chunks):
        for copy in copies[chunk]:
            copy.wait()
        here = slice(chunk * count, (chunk + 1) * count)
        total = (g_ref[here, :].astype(F32) + e_ref[here, :].astype(F32)).astype(BF16)
        for slab in range(cols // LANES):
            first = slab * half + chunk * count
            out_ref[first : first + count, :] = total[:, slab * LANES : (slab + 1) * LANES]


def sent_kernel(core_ref, g_in, e_in, out_ref, *scratch):
    combined_half(1 - core_ref[0], g_in, e_in, out_ref, *scratch)


def kept_kernel(core_ref, g_in, e_in, q_ref, out_ref, p_ref, *scratch):
    combined_half(core_ref[0], g_in, e_in, out_ref, *scratch)
    p_ref[...] = slab_product(out_ref, q_ref, p_ref.shape[0])


def slab_product(slabs_ref, q_ref, half):
    p = jnp.zeros((half, LANES), F32)
    for pair in range(q_ref.shape[0] // (2 * LANES)):
        two = [slabs_ref[(2 * pair + k) * half : (2 * pair + k + 1) * half, :] for k in range(2)]
        q = q_ref[2 * pair * LANES : 2 * (pair + 1) * LANES, :]
        p += jnp.dot(jnp.concatenate(two, axis=1), q, preferred_element_type=F32)
    return p


def half_call(kernel, limit, core, gradient, error, *more):
    rows, cols = gradient.shape
    half = rows // 2
    chunks = 4
    out = jax.ShapeDtypeStruct((cols // LANES * half, LANES), BF16)
    vmem = pl.BlockSpec(memory_space=pltpu.VMEM)
    anywhere = pl.BlockSpec(memory_space=pl.ANY)
    return pl.pallas_call(
        kernel,
        out_shape=(out, jax.ShapeDtypeStruct((half, LANES), F32)) if more else out,
        in_specs=[pl.BlockSpec(memory_space=pltpu.SMEM), anywhere, anywhere] + [vmem] * len(more),
        out_specs=(vmem, vmem) if more else vmem,
        scratch_shapes=[
            pltpu.VMEM((half, cols), BF16),
            pltpu.VMEM((half, cols), BF16),
            pltpu.SemaphoreType.DMA((2, chunks)),
        ],
        compiler_params=pltpu.CompilerParams(vmem_limit_bytes=limit),
        name="kept" if more else "sent",
    )(core, gradient, error, *more)


def pack_kernel(own_ref, got_ref, p_ref, q_ref, out_ref):
    half = p_ref.shape[0]
    span = out_ref.shape[1] - 2 * STEP
    high, low = split(p_ref[...] + slab_product(got_ref, q_ref, half))
    for piece in range(CHIPS):
        if (piece + 1) * STEP <= half:
            out_ref[piece, :STEP, :] = high[piece * STEP : (piece + 1) * STEP, :]
            out_ref[piece, STEP : 2 * STEP, :] = low[piece * STEP : (piece + 1) * STEP, :]
        else:
            out_ref[piece, : 2 * STEP, :] = jnp.zeros((2 * STEP, LANES), BF16)
        first = piece * span
        count = min(span, own_ref.shape[0] - first)
        total = own_ref[first : first + count, :].astype(F32) + got_ref[first : first + count, :].astype(F32)
        out_ref[piece, 2 * STEP : 2 * STEP + count, :] = total.astype(BF16)
        if count < span:
            out_ref[piece, 2 * STEP + count :, :] = jnp.zeros((span - count, LANES), BF16)


def pack(own, got, p_own, q_prev, span):
    return pl.pallas_call(
        pack_kernel,
        out_shape=jax.ShapeDtypeStruct((CHIPS, 2 * STEP + span, LANES), BF16),
        compiler_params=params(),
        name="pack",
    )(own, got, p_own, q_prev)


def sums_kernel(in_ref, left_ref, total_ref):
    left = jnp.zeros(left_ref.shape[1:], F32)
    total = jnp.zeros(total_ref.shape, F32)
    for chip in range(CHIPS):
        left += in_ref[chip, :STEP, :].astype(F32) + in_ref[chip, STEP : 2 * STEP, :].astype(F32)
        total += in_ref[chip, 2 * STEP :, :].astype(F32)
    for copy in range(left_ref.shape[0]):
        left_ref[copy] = left
    total_ref[...] = total.astype(BF16)


def sums(pieces, copies):
    return pl.pallas_call(
        sums_kernel,
        out_shape=(
            jax.ShapeDtypeStruct((copies, STEP, LANES), F32),
            jax.ShapeDtypeStruct((pieces.shape[1] - 2 * STEP, LANES), BF16),
        ),
        compiler_params=params(),
        name="sums",
    )(pieces)


def repack_kernel(left_ref, total_ref, out_ref):
    p = left_ref[0]
    for at in range(1, left_ref.shape[0]):
        p += left_ref[at]
    high, low = split(p)
    total = total_ref[...]
    for chip in range(CHIPS):
        out_ref[chip, :STEP, :] = high
        out_ref[chip, STEP : 2 * STEP, :] = low
        out_ref[chip, 2 * STEP :, :] = total


def repack(left, total):
    return pl.pallas_call(
        repack_kernel,
        out_shape=jax.ShapeDtypeStruct((CHIPS, 2 * STEP + total.shape[0], LANES), BF16),
        compiler_params=params(),
        name="repack",
    )(left, total)


def spread(x, row=None, lane=None):
    if row is not None:
        x = x[row : row + 1, :]
    if lane is not None:
        x = x[:, lane : lane + 1]
    return jnp.broadcast_to(x, (8, LANES))


def inverse_factor(gram):
    width = 8
    groups = LANES // width
    w = [gram[width * g : width * (g + 1), :] for g in range(groups)]
    row_of = lax.broadcasted_iota(jnp.int32, (width, LANES), 0)
    lane_of = lax.broadcasted_iota(jnp.int32, (width, LANES), 1)
    for g in range(groups):
        first = width * g
        column = {h: [spread(w[h], lane=first + i) for i in range(width)] for h in range(g, groups)}
        inside = (lane_of >= first) & (lane_of < first + width)
        start = jnp.where(inside, jnp.where(lane_of - first == row_of, 1.0, 0.0), w[g])
        y = [spread(start, row=m) for m in range(width)]
        d = [[spread(column[g][i], row=m) for i in range(m + 1)] for m in range(width)]
        low = [[None] * width for _ in range(width)]
        root = [None] * width
        lead = list(column[g + 1]) if g + 1 < groups else None
        for i in range(width):
            if i % 2 == 0:
                first_root = lax.rsqrt(d[i][i])
                det = d[i][i] * d[i + 1][i + 1] - d[i + 1][i] * d[i + 1][i]
                root[i] = first_root
                root[i + 1] = d[i][i] * first_root * lax.rsqrt(det)
            for m in range(i + 1, width):
                low[m][i] = d[m][i] * root[i]
            for m in range(i + 1, width):
                for n in range(i + 1, m + 1):
                    if i % 2 == 1 or m > i + 1:
                        d[m][n] = d[m][n] - low[m][i] * low[n][i]
            y[i] = y[i] * root[i]
            for m in range(i + 1, width):
                y[m] = y[m] - low[m][i] * y[i]
            if lead is not None:
                lead[i] = lead[i] * root[i]
                for m in range(i + 1, width):
                    lead[m] = lead[m] - low[m][i] * lead[i]
        z = [None] * width
        for m in reversed(range(width)):
            value = y[m]
            for k in range(m + 1, width):
                value = value - low[k][m] * z[k]
            z[m] = value * root[m]
        for h in range(g + 1, groups):
            left, right = (lead, y) if h == g + 1 else (column[h], z)
            terms = [left[i] * right[i] for i in range(width)]
            while len(terms) > 1:
                terms = [terms[i] + terms[i + 1] for i in range(0, len(terms), 2)]
            w[h] = jnp.where(inside, 0.0, w[h]) - terms[0]
        rows = y[0]
        for m in range(1, width):
            rows = jnp.where(row_of == m, y[m], rows)
        w[g] = jnp.where(lane_of <= row_of + first, rows, 0.0)
    return jnp.concatenate(w, axis=0)


def basis_kernel(own_ref, other_ref, out_ref):
    half = out_ref.shape[1]

    def left_half(ref):
        parts = [
            ref[piece, :STEP, :].astype(F32) + ref[piece, STEP : 2 * STEP, :].astype(F32)
            for piece in range(half // STEP)
        ]
        return jnp.concatenate(parts, axis=0)

    def product(x, y, dims):
        return lax.dot_general(
            x, y, (dims, ((), ())), precision=lax.Precision.HIGHEST, preferred_element_type=F32
        )

    halves = left_half(own_ref), left_half(other_ref)
    squares = [jnp.sum(p * p, axis=0, keepdims=True) for p in halves]
    scale = lax.rsqrt(squares[0] + squares[1])
    halves = [p * scale for p in halves]
    grams = [product(p, p, ((0,), (0,))) for p in halves]
    inverse = inverse_factor(grams[0] + grams[1])
    for at, p in enumerate(halves):
        out_ref[at] = product(p, inverse, ((1,), (1,))).astype(BF16)


def bases(own, other, half):
    return pl.pallas_call(
        basis_kernel,
        out_shape=jax.ShapeDtypeStruct((2, half, LANES), BF16),
        compiler_params=params(),
        name="basis",
    )(own, other)


def finish_kernel(
    replicas,
    core_ref,
    own_ref,
    other_ref,
    own_sum_ref,
    other_sum_ref,
    basis_ref,
    error_out,
    q_out,
    error_ref,
    q_ref,
    sems,
):
    core = core_ref[0]
    half = basis_ref.shape[1]
    span = own_sum_ref.shape[1] - 2 * STEP

    def slab_of(ref, slab):
        at, end, parts = slab * half, (slab + 1) * half, []
        while at < end:
            piece = at // span
            stop = min(end, (piece + 1) * span)
            parts.append(ref[piece, 2 * STEP + at - piece * span : 2 * STEP + stop - piece * span, :])
            at = stop
        return jnp.concatenate(parts, axis=0)

    def pair_of(read, pair):
        return jnp.concatenate([read(2 * pair), read(2 * pair + 1)], axis=1)

    basis = (basis_ref[0], basis_ref[1])
    flipped = [b.astype(F32).T.astype(BF16) for b in basis]
    copies = []
    for pair in range(q_ref.shape[0] // (2 * LANES)):
        columns = slice(2 * pair * LANES, 2 * (pair + 1) * LANES)
        terms = [
            jnp.dot(flat, pair_of(lambda slab: slab_of(ref, slab), pair), preferred_element_type=F32)
            for flat, ref in zip(flipped, (own_sum_ref, other_sum_ref))
        ]
        scaled = (terms[0] + terms[1]) * (1.0 / replicas)
        q_ref[columns, :] = scaled.T.astype(BF16)
        right = scaled.astype(BF16)
        for which, ref, b in ((core, own_ref, basis[0]), (1 - core, other_ref, basis[1])):
            mine = pair_of(lambda slab: ref[slab * half : (slab + 1) * half, :], pair).astype(F32)
            rows = pl.ds(pl.multiple_of(which * half, half), half)
            error_ref[rows, columns] = (mine - jnp.dot(b, right, preferred_element_type=F32)).astype(BF16)
        copies += [
            pltpu.make_async_copy(q_ref.at[columns, :], q_out.at[columns, :], sems.at[0, pair]),
            pltpu.make_async_copy(error_ref.at[:, columns], error_out.at[:, columns], sems.at[1, pair]),
        ]
        for copy in copies[-2:]:
            copy.start()
    for copy in copies:
        copy.wait()


def finish(core, own, other, own_sum, other_sum, basis, replicas):
    rows, cols = 2 * basis.shape[1], own.shape[0] // basis.shape[1] * LANES
    vmem = pl.BlockSpec(memory_space=pltpu.VMEM)
    return pl.pallas_call(
        lambda *refs: finish_kernel(replicas, *refs),
        out_shape=(jax.ShapeDtypeStruct((rows, cols), BF16), jax.ShapeDtypeStruct((cols, LANES), BF16)),
        in_specs=[pl.BlockSpec(memory_space=pltpu.SMEM)] + [vmem] * 5,
        out_specs=(pl.BlockSpec(memory_space=pl.ANY),) * 2,
        scratch_shapes=[
            pltpu.VMEM((rows, cols), BF16),
            pltpu.VMEM((cols, LANES), BF16),
            pltpu.SemaphoreType.DMA((2, cols // (2 * LANES))),
        ],
        compiler_params=params(),
        name="finish",
    )(core, own, other, own_sum, other_sum, basis)


def on_device(gradient, error, q_prev):
    rows, cols = gradient.shape[1:]
    replicas = lax.axis_size("dp")
    half = rows // 2
    slab_rows = cols // LANES * half
    span = -(-slab_rows // CHIPS // 16) * 16
    core = (lax.axis_index("dp") % 2).astype(jnp.int32).reshape(1)
    twin = [(i, i ^ 1) for i in range(replicas)]
    same_core = [[2 * chip + c for chip in range(CHIPS)] for c in range(2)]

    def across_chips(pieces):
        return lax.all_to_all(pieces, "dp", 0, 0, axis_index_groups=same_core)

    other = half_call(sent_kernel, SENT_LIMIT, core, gradient[0], error[0])
    got = lax.ppermute(other, "dp", twin)
    own, p_own = half_call(kept_kernel, KEPT_LIMIT, core, gradient[0], error[0], q_prev)
    pieces = across_chips(pack(own, got, p_own, q_prev, span))
    left, total = sums(pieces, lax.axis_size("tensor"))
    left = lax.all_to_all(left, "tensor", 0, 0)
    gathered = across_chips(repack(left, total))
    gathered_other = lax.ppermute(gathered, "dp", twin)
    basis = bases(gathered, gathered_other, half)
    new_error, q_next = finish(core, own, other, gathered, gathered_other, basis, replicas)
    return (new_error[None], q_next)


def solution(mesh):
    placed = (P("dp", None, "tensor"), P("dp", None, "tensor"), P("tensor", None))
    return jax.shard_map(
        on_device,
        mesh=mesh,
        in_specs=placed,
        out_specs=(P("dp", None, "tensor"), P("tensor", None)),
        check_vma=False,
    )
```

time: 640 us -> 86.6 us (0.14)
  waiting for transfers between devices: 591 us -> 1.99 us
  blocking collectives: 0 us -> 57 us
  other arithmetic: 24.1 us -> 0 us
  starting transfers between devices: 0.08 us -> 15.3 us
  between operations: 14.1 us -> 0.72 us
  Pallas kernels: 0 us -> 11.3 us
  matrix products: 8.94 us -> 0 us
    psum x2 -> x0, waiting for transfers between devices: 591 us -> none  [the longest x1 462 us: on_device(): p_sum = lax.psum(p_local, ('dp', 'tensor'))]
    all_to_all x0 -> x3, blocking collectives: none -> 57 us  [the longest x2 31.7 us: across_chips(): return lax.all_to_all(pieces, 'dp', 0, 0, axis_index_groups=same_core)]
    another operation x5 -> x0, other arithmetic: 22.9 us -> none  [the longest x3 12.4 us: orthonormal(): lower = jnp.linalg.cholesky(gram)]
    ppermute x0 -> x2, starting transfers between devices: none -> 15.3 us  [the longest x1 8.79 us: on_device(): got = lax.ppermute(other, 'dp', twin)]
    pallas_call x0 -> x7, Pallas kernels: none -> 11.3 us  [the longest x1 4.59 us: bases(): pl.pallas_call(basis_kernel, out_shape=jax.ShapeDtypeStruct((2, half, LAN...]
    dot_general x4 -> x0, matrix products: 7.7 us -> none  [the longest x1 3.08 us: on_device(): p_local = jnp.dot(combined, q_prev, preferred_element_type=jnp.float32)]
  transfers between devices with their start and end apart: 2 -> 2, of which waited for: 2 -> 1; matrix products, arithmetic and copies ran while one was open for 0% -> 0% of each run, Pallas kernels for 0% -> 2%
where the time goes in v3:
time: 86.6 us; the launch traced here: 86.3 us
  blocking collectives  57 us (66%)
  starting transfers between devices  15.3 us (18%)
  Pallas kernels  11.3 us (13%)
  waiting for transfers between devices  1.99 us (2%)
    all_to_all x2, blocking collectives, across_chips(): return lax.all_to_all(pieces, 'dp', 0, 0, axis_index_groups=same_core)  31.7 us
    all_to_all x1, blocking collectives, on_device(): left = lax.all_to_all(left, 'tensor', 0, 0)  25.3 us
    ppermute x1, starting transfers between devices, on_device(): got = lax.ppermute(other, 'dp', twin)  8.79 us
    ppermute x1, starting transfers between devices, on_device(): gathered_other = lax.ppermute(gathered, 'dp', twin)  6.53 us
    pallas_call x1, Pallas kernels, bases(): pl.pallas_call(basis_kernel, out_shape=jax.ShapeDtypeStruct((2, half, LAN...  4.59 us
    pallas_call x2, Pallas kernels, half_call(): pl.pallas_call(kernel, out_shape=(out, jax.ShapeDtypeStruct((half, LANES)...  3.42 us
    pallas_call x1, Pallas kernels, finish(): pl.pallas_call(lambda *refs: finish_kernel(replicas, *refs), out_shape=(j...  2.62 us
    ppermute x1, waiting for transfers between devices, on_device(): gathered_other = lax.ppermute(gathered, 'dp', twin)  1.98 us
  transfers between devices with their start and end apart: 2, of which 1 were waited for; matrix products, arithmetic and copies ran while one was open for 0% of the time, Pallas kernels for 2%

profile of v3, /device:TPU:1, one launch (start us, length us, event | category | flops | bytes accessed | tf_op | source)
XLA Modules:
  0.0 86.3 jit_solution(9018943934244913748)
XLA Ops:
  0.6 0.0 copy-start
  0.7 1.6 %sent.1.refs_2_ = bf16[2688,128]{1,0:T(8,128)(2,1)S(1)} custom-call(s32[1]{0:T(128)} %bitcast.core_ref.refs_0_, bf16[384,1792]{1,0:T(8,128)(2,1)} %bitcast.4, bf16[384,1792]{1,0:T(8,128)(2,1)} %bitcast.6), custom_call_target="tpu_custom_call" | custom-call | tf_op jit(solution)/shard_map/sent/pallas_call | solution.py:76
  2.2 8.8 %collective-permute-start = (bf16[2688,128]{1,0:T(8,128)(2,1)S(1)}, bf16[2688,128]{1,0:T(8,128)(2,1)S(1)}, u32[]{:S(2)}, u32[]{:S(2)}) collective-permute-start(bf16[2688,128]{1,0:T(8,128)(2,1)S(1)} %sent.1.refs_2_), channel_id=1, source_target_pairs={{0,16},{16,0},{32,48},{48,32},{64,80},{80,64},{96,112},{112,96},{1... | collective-permute-start | bytes 2064392 | tf_op jit(solution)/shard_map/ppermute | solution.py:346
  11.0 0.0 copy-done
  11.0 1.9 %kept.1 = (bf16[2688,128]{1,0:T(8,128)(2,1)S(1)}, f32[192,128]{1,0:T(8,128)S(1)}) custom-call(s32[1]{0:T(128)} %bitcast.core_ref.refs_0_, bf16[384,1792]{1,0:T(8,128)(2,1)} %bitcast.5, bf16[384,1792]{1,0:T(8,128)(2,1)} %bitcast.7, bf16[1792,128]{1,0:T(8,128)(2,1)S(1)} %copy-done), custom_call_target="tpu_custom_call" | custom-call | tf_op jit(solution)/shard_map/kept/pallas_call | solution.py:76
  12.9 0.0 collective-permute-done.got_ref
  12.9 0.4 pack.1
  13.3 17.3 %all_to_all.15.in_ref = bf16[16,208,128]{2,1,0:T(8,128)(2,1)S(1)} all-to-all(bf16[16,208,128]{2,1,0:T(8,128)(2,1)S(1)} %pack.1), channel_id=1, replica_groups={{0,32,64,96,128,160,192,224,256,288,320,352,384,416,448,480},{16,48,80,..., dimensions={0} | all-to-all | bytes 1703936 | tf_op jit(solution)/shard_map/all_to_all | solution.py:343
  30.6 0.1 sums.1
  30.7 25.3 %all_to_all.16.left_ref = f32[16,16,128]{2,1,0:T(8,128)S(1)} all-to-all(f32[16,16,128]{2,1,0:T(8,128)S(1)} %get-tuple-element.10), channel_id=1, replica_groups=mesh['dp'=32,'tensor'=16] {'tensor'}, dimensions={0} | all-to-all | bytes 262144 | tf_op jit(solution)/shard_map/all_to_all | solution.py:350
  56.0 0.1 repack.1
  56.1 14.4 %all_to_all.17.own_ref.refs_3_ = bf16[16,208,128]{2,1,0:T(8,128)(2,1)S(1)} all-to-all(bf16[16,208,128]{2,1,0:T(8,128)(2,1)S(1)} %repack.1), channel_id=1, replica_groups={{0,32,64,96,128,160,192,224,256,288,320,352,384,416,448,480},{16,48,80,..., dimensions={0} | all-to-all | bytes 1703936 | tf_op jit(solution)/shard_map/all_to_all | solution.py:343
  70.5 6.5 %collective-permute-start.1 = (bf16[16,208,128]{2,1,0:T(8,128)(2,1)S(1)}, bf16[16,208,128]{2,1,0:T(8,128)(2,1)S(1)}, u32[]{:S(2)}, u32[]{:S(2)}) collective-permute-start(bf16[16,208,128]{2,1,0:T(8,128)(2,1)S(1)} %all_to_all.17.own_ref.refs_3_), channel_id=1, source_target_pairs={{0,16},{16,0},{32,48},{48,32},{64,80},{80,64},{96,112},{112,96},{1... | collective-permute-start | bytes 2555912 | tf_op jit(solution)/shard_map/ppermute | solution.py:352
  77.1 2.0 %collective-permute-done.1.other_ref.refs_4_ = bf16[16,208,128]{2,1,0:T(8,128)(2,1)S(1)} collective-permute-done((bf16[16,208,128]{2,1,0:T(8,128)(2,1)S(1)}, bf16[16,208,128]{2,1,0:T(8,128)(2,1)S(1)}, u32[]{:S(2)}, u32[]{:S(2)}) %collective-permute-start.1) | collective-permute-done | bytes 852000 | tf_op jit(solution)/shard_map/ppermute | solution.py:352
  79.0 4.6 %basis.1.refs_5_ = bf16[2,192,128]{2,1,0:T(8,128)(2,1)S(1)} custom-call(bf16[16,208,128]{2,1,0:T(8,128)(2,1)S(1)} %all_to_all.17.own_ref.refs_3_, bf16[16,208,128]{2,1,0:T(8,128)(2,1)S(1)} %collective-permute-done.1.other_ref.refs_4_), custom_call_target="tpu_custom_call" | custom-call | tf_op jit(solution)/shard_map/basis/pallas_call | solution.py:250
  83.7 2.6 %finish.1 = (bf16[384,1792]{1,0:T(8,128)(2,1)}, bf16[1792,128]{1,0:T(8,128)(2,1)}) custom-call(s32[1]{0:T(128)} %bitcast.core_ref.refs_0_, bf16[2688,128]{1,0:T(8,128)(2,1)S(1)} %get-tuple-element.8.own_ref.refs_1_, bf16[2688,128]{1,0:T(8,128)(2,1)S(1)} %sent.1.refs_2_, bf16[16,208,128]{2,1,0:T(8,128)(2,1)S(1)} %all_to_all.17.own_ref.refs_3_, ...), custom_call_target="tpu_custom_call" | custom-call | tf_op jit(solution)/shard_map/finish/pallas_call | solution.py:317
Async XLA Ops:
  0.6 10.4 %copy-start = (bf16[1792,128]{1,0:T(8,128)(2,1)S(1)}, bf16[1792,128]{1,0:T(8,128)(2,1)}, u32[]{:S(2)}) copy-start(bf16[1792,128]{1,0:T(8,128)(2,1)} %q_ref.3) | copy-start | bytes 1376260
  2.2 10.7 %collective-permute-start = (bf16[2688,128]{1,0:T(8,128)(2,1)S(1)}, bf16[2688,128]{1,0:T(8,128)(2,1)S(1)}, u32[]{:S(2)}, u32[]{:S(2)}) collective-permute-start(bf16[2688,128]{1,0:T(8,128)(2,1)S(1)} %sent.1.refs_2_), channel_id=1, source_target_pairs={{0,16},{16,0},{32,48},{48,32},{64,80},{80,64},{96,112},{112,96},{1... | collective-permute-start | bytes 2064392 | tf_op jit(solution)/shard_map/ppermute | solution.py:346
  70.5 8.5 %collective-permute-start.1 = (bf16[16,208,128]{2,1,0:T(8,128)(2,1)S(1)}, bf16[16,208,128]{2,1,0:T(8,128)(2,1)S(1)}, u32[]{:S(2)}, u32[]{:S(2)}) collective-permute-start(bf16[16,208,128]{2,1,0:T(8,128)(2,1)S(1)} %all_to_all.17.own_ref.refs_3_), channel_id=1, source_target_pairs={{0,16},{16,0},{32,48},{48,32},{64,80},{80,64},{96,112},{112,96},{1... | collective-permute-start | bytes 2555912 | tf_op jit(solution)/shard_map/ppermute | solution.py:352

commit v4 on v3

--- a/solution.py
+++ b/solution.py
@@ -8,7 +8,8 @@
 F32, BF16 = jnp.float32, jnp.bfloat16
 LANES = 128
 CHIPS = 16
-STEP = 16
+MAIN = 160
+MIXED = 32
 VMEM_LIMIT = 48 * 1024 * 1024
 SENT_LIMIT = 52 * 1024 * 1024
 KEPT_LIMIT = 52 * 1024 * 1024
@@ -16,11 +17,6 @@
 
 def params():
     return pltpu.CompilerParams(vmem_limit_bytes=VMEM_LIMIT)
-
-
-def split(x):
-    high = x.astype(BF16)
-    return high, (x - high.astype(F32)).astype(BF16)
 
 
 def combined_half(which, g_in, e_in, out_ref, g_ref, e_ref, sems):
@@ -69,7 +65,7 @@
 def half_call(kernel, limit, core, gradient, error, *more):
     rows, cols = gradient.shape
     half = rows // 2
-    chunks = 4
+    chunks = 2
     out = jax.ShapeDtypeStruct((cols // LANES * half, LANES), BF16)
     vmem = pl.BlockSpec(memory_space=pltpu.VMEM)
     anywhere = pl.BlockSpec(memory_space=pl.ANY)
@@ -88,50 +84,69 @@
     )(core, gradient, error, *more)
 
 
+def upper_rows():
+    return lax.broadcasted_iota(jnp.int32, (8, LANES), 0) < 4
+
+
+def swap(x):
+    return jnp.concatenate([x[4:, :], x[:4, :]], axis=0)
+
+
+def high_low(x):
+    high = x.astype(BF16).astype(F32)
+    return high, x - high
+
+
+def joined(eight, four):
+    high, low = high_low(eight)
+    high4, low4 = high_low(four)
+    return jnp.concatenate([high, low, jnp.where(upper_rows(), high4, low4)], axis=0)
+
+
+def parted(x):
+    return x[:8, :] + x[8:16, :], x[16:, :] + swap(x[16:, :])
+
+
 def pack_kernel(own_ref, got_ref, p_ref, q_ref, out_ref):
     half = p_ref.shape[0]
-    span = out_ref.shape[1] - 2 * STEP
-    high, low = split(p_ref[...] + slab_product(got_ref, q_ref, half))
+    p = p_ref[...] + slab_product(got_ref, q_ref, half)
     for piece in range(CHIPS):
-        if (piece + 1) * STEP <= half:
-            out_ref[piece, :STEP, :] = high[piece * STEP : (piece + 1) * STEP, :]
-            out_ref[piece, STEP : 2 * STEP, :] = low[piece * STEP : (piece + 1) * STEP, :]
-        else:
-            out_ref[piece, : 2 * STEP, :] = jnp.zeros((2 * STEP, LANES), BF16)
-        first = piece * span
-        count = min(span, own_ref.shape[0] - first)
-        total = own_ref[first : first + count, :].astype(F32) + got_ref[first : first + count, :].astype(F32)
-        out_ref[piece, 2 * STEP : 2 * STEP + count, :] = total.astype(BF16)
-        if count < span:
-            out_ref[piece, 2 * STEP + count :, :] = jnp.zeros((span - count, LANES), BF16)
-
-
-def pack(own, got, p_own, q_prev, span):
+        rows = slice(piece * MAIN, (piece + 1) * MAIN)
+        out_ref[piece, :MAIN, :] = (own_ref[rows, :].astype(F32) + got_ref[rows, :].astype(F32)).astype(BF16)
+    last = slice(CHIPS * MAIN, CHIPS * (MAIN + 8))
+    extra = own_ref[last, :].astype(F32) + got_ref[last, :].astype(F32)
+    for piece in range(CHIPS):
+        both = p[8 * (CHIPS + piece // 2) : 8 * (CHIPS + piece // 2 + 1), :]
+        four = jnp.where(upper_rows() == (piece % 2 == 0), both, swap(both))
+        mixed = [extra[8 * piece : 8 * piece + 8, :], joined(p[8 * piece : 8 * piece + 8, :], four)]
+        out_ref[piece, MAIN:, :] = jnp.concatenate(mixed, axis=0).astype(BF16)
+
+
+def pack(own, got, p_own, q_prev):
     return pl.pallas_call(
         pack_kernel,
-        out_shape=jax.ShapeDtypeStruct((CHIPS, 2 * STEP + span, LANES), BF16),
+        out_shape=jax.ShapeDtypeStruct((CHIPS, MAIN + MIXED, LANES), BF16),
         compiler_params=params(),
         name="pack",
     )(own, got, p_own, q_prev)
 
 
 def sums_kernel(in_ref, left_ref, total_ref):
-    left = jnp.zeros(left_ref.shape[1:], F32)
-    total = jnp.zeros(total_ref.shape, F32)
-    for chip in range(CHIPS):
-        left += in_ref[chip, :STEP, :].astype(F32) + in_ref[chip, STEP : 2 * STEP, :].astype(F32)
-        total += in_ref[chip, 2 * STEP :, :].astype(F32)
+    total = in_ref[0].astype(F32)
+    for chip in range(1, CHIPS):
+        total += in_ref[chip].astype(F32)
+    left = joined(*parted(total[MAIN + 8 :, :])).astype(BF16)
     for copy in range(left_ref.shape[0]):
         left_ref[copy] = left
-    total_ref[...] = total.astype(BF16)
+    total_ref[...] = total[: MAIN + 8, :]
 
 
 def sums(pieces, copies):
     return pl.pallas_call(
         sums_kernel,
         out_shape=(
-            jax.ShapeDtypeStruct((copies, STEP, LANES), F32),
-            jax.ShapeDtypeStruct((pieces.shape[1] - 2 * STEP, LANES), BF16),
+            jax.ShapeDtypeStruct((copies, MIXED - 8, LANES), BF16),
+            jax.ShapeDtypeStruct((MAIN + 8, LANES), F32),
         ),
         compiler_params=params(),
         name="sums",
@@ -139,21 +154,18 @@
 
 
 def repack_kernel(left_ref, total_ref, out_ref):
-    p = left_ref[0]
+    left = left_ref[0].astype(F32)
     for at in range(1, left_ref.shape[0]):
-        p += left_ref[at]
-    high, low = split(p)
-    total = total_ref[...]
+        left += left_ref[at].astype(F32)
+    piece = jnp.concatenate([total_ref[...], joined(*parted(left))], axis=0).astype(BF16)
     for chip in range(CHIPS):
-        out_ref[chip, :STEP, :] = high
-        out_ref[chip, STEP : 2 * STEP, :] = low
-        out_ref[chip, 2 * STEP :, :] = total
+        out_ref[chip] = piece
 
 
 def repack(left, total):
     return pl.pallas_call(
         repack_kernel,
-        out_shape=jax.ShapeDtypeStruct((CHIPS, 2 * STEP + total.shape[0], LANES), BF16),
+        out_shape=jax.ShapeDtypeStruct((CHIPS, MAIN + MIXED, LANES), BF16),
         compiler_params=params(),
         name="repack",
     )(left, total)
@@ -225,11 +237,9 @@
     half = out_ref.shape[1]
 
     def left_half(ref):
-        parts = [
-            ref[piece, :STEP, :].astype(F32) + ref[piece, STEP : 2 * STEP, :].astype(F32)
-            for piece in range(half // STEP)
-        ]
-        return jnp.concatenate(parts, axis=0)
+        parts = [parted(ref[piece, MAIN:, :].astype(F32)[8:, :]) for piece in range(CHIPS)]
+        lower = [jnp.where(upper_rows(), parts[2 * k][1], parts[2 * k + 1][1]) for k in range(CHIPS // 2)]
+        return jnp.concatenate([eight for eight, _ in parts] + lower, axis=0)
 
     def product(x, y, dims):
         return lax.dot_general(
@@ -271,15 +281,17 @@
 ):
     core = core_ref[0]
     half = basis_ref.shape[1]
-    span = own_sum_ref.shape[1] - 2 * STEP
 
     def slab_of(ref, slab):
         at, end, parts = slab * half, (slab + 1) * half, []
-        while at < end:
-            piece = at // span
-            stop = min(end, (piece + 1) * span)
-            parts.append(ref[piece, 2 * STEP + at - piece * span : 2 * STEP + stop - piece * span, :])
+        while at < min(end, CHIPS * MAIN):
+            piece = at // MAIN
+            stop = min(end, (piece + 1) * MAIN)
+            parts.append(ref[piece, at - piece * MAIN : stop - piece * MAIN, :])
             at = stop
+        if at < end:
+            extra = [ref[piece, MAIN : MAIN + 16, :].astype(F32)[:8, :] for piece in range(CHIPS)]
+            parts.append(jnp.concatenate(extra, axis=0).astype(BF16))
         return jnp.concatenate(parts, axis=0)
 
     def pair_of(read, pair):
@@ -333,8 +345,6 @@
     rows, cols = gradient.shape[1:]
     replicas = lax.axis_size("dp")
     half = rows // 2
-    slab_rows = cols // LANES * half
-    span = -(-slab_rows // CHIPS // 16) * 16
     core = (lax.axis_index("dp") % 2).astype(jnp.int32).reshape(1)
     twin = [(i, i ^ 1) for i in range(replicas)]
     same_core = [[2 * chip + c for chip in range(CHIPS)] for c in range(2)]
@@ -345,7 +355,7 @@
     other = half_call(sent_kernel, SENT_LIMIT, core, gradient[0], error[0])
     got = lax.ppermute(other, "dp", twin)
     own, p_own = half_call(kept_kernel, KEPT_LIMIT, core, gradient[0], error[0], q_prev)
-    pieces = across_chips(pack(own, got, p_own, q_prev, span))
+    pieces = across_chips(pack(own, got, p_own, q_prev))
     left, total = sums(pieces, lax.axis_size("tensor"))
     left = lax.all_to_all(left, "tensor", 0, 0)
     gathered = across_chips(repack(left, total))

time: 86.6 us -> 84.6 us (0.977)
  blocking collectives: 57 us -> 56 us
where the time goes in v4:
time: 84.6 us; the launch traced here: 84.3 us
  blocking collectives  56 us (66%)
  starting transfers between devices  14.7 us (17%)
  Pallas kernels  11 us (13%)
  waiting for transfers between devices  1.91 us (2%)
    all_to_all x2, blocking collectives, across_chips(): return lax.all_to_all(pieces, 'dp', 0, 0, axis_index_groups=same_core)  31.1 us
    all_to_all x1, blocking collectives, on_device(): left = lax.all_to_all(left, 'tensor', 0, 0)  25 us
    ppermute x1, starting transfers between devices, on_device(): got = lax.ppermute(other, 'dp', twin)  8.79 us
    ppermute x1, starting transfers between devices, on_device(): gathered_other = lax.ppermute(gathered, 'dp', twin)  5.88 us
    pallas_call x1, Pallas kernels, bases(): pl.pallas_call(basis_kernel, out_shape=jax.ShapeDtypeStruct((2, half, LAN...  4.6 us
    pallas_call x2, Pallas kernels, half_call(): pl.pallas_call(kernel, out_shape=(out, jax.ShapeDtypeStruct((half, LANES)...  3.17 us
    pallas_call x1, Pallas kernels, finish(): pl.pallas_call(lambda *refs: finish_kernel(replicas, *refs), out_shape=(j...  2.62 us
    ppermute x1, waiting for transfers between devices, on_device(): gathered_other = lax.ppermute(gathered, 'dp', twin)  1.89 us
  transfers between devices with their start and end apart: 2, of which 1 were waited for; matrix products, arithmetic and copies ran while one was open for 0% of the time, Pallas kernels for 2%

profile of v4, /device:TPU:1, one launch (start us, length us, event | category | flops | bytes accessed | tf_op | source)
XLA Modules:
  0.0 84.3 jit_solution(5549745897335054444)
XLA Ops:
  0.6 0.0 copy-start
  0.7 1.5 %sent.1.refs_2_ = bf16[2688,128]{1,0:T(8,128)(2,1)S(1)} custom-call(s32[1]{0:T(128)} %bitcast.core_ref.refs_0_, bf16[384,1792]{1,0:T(8,128)(2,1)} %bitcast.4, bf16[384,1792]{1,0:T(8,128)(2,1)} %bitcast.6), custom_call_target="tpu_custom_call" | custom-call | tf_op jit(solution)/shard_map/sent/pallas_call | solution.py:72
  2.1 8.8 %collective-permute-start = (bf16[2688,128]{1,0:T(8,128)(2,1)S(1)}, bf16[2688,128]{1,0:T(8,128)(2,1)S(1)}, u32[]{:S(2)}, u32[]{:S(2)}) collective-permute-start(bf16[2688,128]{1,0:T(8,128)(2,1)S(1)} %sent.1.refs_2_), channel_id=1, source_target_pairs={{0,16},{16,0},{32,48},{48,32},{64,80},{80,64},{96,112},{112,96},{1... | collective-permute-start | bytes 2064392 | tf_op jit(solution)/shard_map/ppermute | solution.py:356
  10.9 0.0 copy-done
  10.9 1.7 %kept.1 = (bf16[2688,128]{1,0:T(8,128)(2,1)S(1)}, f32[192,128]{1,0:T(8,128)S(1)}) custom-call(s32[1]{0:T(128)} %bitcast.core_ref.refs_0_, bf16[384,1792]{1,0:T(8,128)(2,1)} %bitcast.5, bf16[384,1792]{1,0:T(8,128)(2,1)} %bitcast.7, bf16[1792,128]{1,0:T(8,128)(2,1)S(1)} %copy-done), custom_call_target="tpu_custom_call" | custom-call | tf_op jit(solution)/shard_map/kept/pallas_call | solution.py:72
  12.6 0.0 collective-permute-done.got_ref
  12.7 0.4 pack.1
  13.1 16.7 %all_to_all.15.in_ref = bf16[16,192,128]{2,1,0:T(8,128)(2,1)S(1)} all-to-all(bf16[16,192,128]{2,1,0:T(8,128)(2,1)S(1)} %pack.1), channel_id=1, replica_groups={{0,32,64,96,128,160,192,224,256,288,320,352,384,416,448,480},{16,48,80,..., dimensions={0} | all-to-all | bytes 1572864 | tf_op jit(solution)/shard_map/all_to_all | solution.py:353
  29.8 0.1 sums.1
  29.9 25.0 %all_to_all.16.left_ref = bf16[16,24,128]{2,1,0:T(8,128)(2,1)S(1)} all-to-all(bf16[16,24,128]{2,1,0:T(8,128)(2,1)S(1)} %get-tuple-element.10), channel_id=1, replica_groups=mesh['dp'=32,'tensor'=16] {'tensor'}, dimensions={0} | all-to-all | bytes 196608 | tf_op jit(solution)/shard_map/all_to_all | solution.py:360
  54.9 0.1 repack.1
  55.0 14.4 %all_to_all.17.own_ref.refs_3_ = bf16[16,192,128]{2,1,0:T(8,128)(2,1)S(1)} all-to-all(bf16[16,192,128]{2,1,0:T(8,128)(2,1)S(1)} %repack.1), channel_id=1, replica_groups={{0,32,64,96,128,160,192,224,256,288,320,352,384,416,448,480},{16,48,80,..., dimensions={0} | all-to-all | bytes 1572864 | tf_op jit(solution)/shard_map/all_to_all | solution.py:353
  69.3 5.9 %collective-permute-start.1 = (bf16[16,192,128]{2,1,0:T(8,128)(2,1)S(1)}, bf16[16,192,128]{2,1,0:T(8,128)(2,1)S(1)}, u32[]{:S(2)}, u32[]{:S(2)}) collective-permute-start(bf16[16,192,128]{2,1,0:T(8,128)(2,1)S(1)} %all_to_all.17.own_ref.refs_3_), channel_id=1, source_target_pairs={{0,16},{16,0},{32,48},{48,32},{64,80},{80,64},{96,112},{112,96},{1... | collective-permute-start | bytes 2359304 | tf_op jit(solution)/shard_map/ppermute | solution.py:362
  75.2 1.9 %collective-permute-done.1.other_ref.refs_4_ = bf16[16,192,128]{2,1,0:T(8,128)(2,1)S(1)} collective-permute-done((bf16[16,192,128]{2,1,0:T(8,128)(2,1)S(1)}, bf16[16,192,128]{2,1,0:T(8,128)(2,1)S(1)}, u32[]{:S(2)}, u32[]{:S(2)}) %collective-permute-start.1) | collective-permute-done | bytes 786464 | tf_op jit(solution)/shard_map/ppermute | solution.py:362
  77.1 4.6 %basis.1.refs_5_ = bf16[2,192,128]{2,1,0:T(8,128)(2,1)S(1)} custom-call(bf16[16,192,128]{2,1,0:T(8,128)(2,1)S(1)} %all_to_all.17.own_ref.refs_3_, bf16[16,192,128]{2,1,0:T(8,128)(2,1)S(1)} %collective-permute-done.1.other_ref.refs_4_), custom_call_target="tpu_custom_call" | custom-call | tf_op jit(solution)/shard_map/basis/pallas_call | solution.py:260
  81.7 2.6 %finish.1 = (bf16[384,1792]{1,0:T(8,128)(2,1)}, bf16[1792,128]{1,0:T(8,128)(2,1)}) custom-call(s32[1]{0:T(128)} %bitcast.core_ref.refs_0_, bf16[2688,128]{1,0:T(8,128)(2,1)S(1)} %get-tuple-element.8.own_ref.refs_1_, bf16[2688,128]{1,0:T(8,128)(2,1)S(1)} %sent.1.refs_2_, bf16[16,192,128]{2,1,0:T(8,128)(2,1)S(1)} %all_to_all.17.own_ref.refs_3_, ...), custom_call_target="tpu_custom_call" | custom-call | tf_op jit(solution)/shard_map/finish/pallas_call | solution.py:329
Async XLA Ops:
  0.6 10.3 %copy-start = (bf16[1792,128]{1,0:T(8,128)(2,1)S(1)}, bf16[1792,128]{1,0:T(8,128)(2,1)}, u32[]{:S(2)}) copy-start(bf16[1792,128]{1,0:T(8,128)(2,1)} %q_ref.3) | copy-start | bytes 1376260
  2.1 10.5 %collective-permute-start = (bf16[2688,128]{1,0:T(8,128)(2,1)S(1)}, bf16[2688,128]{1,0:T(8,128)(2,1)S(1)}, u32[]{:S(2)}, u32[]{:S(2)}) collective-permute-start(bf16[2688,128]{1,0:T(8,128)(2,1)S(1)} %sent.1.refs_2_), channel_id=1, source_target_pairs={{0,16},{16,0},{32,48},{48,32},{64,80},{80,64},{96,112},{112,96},{1... | collective-permute-start | bytes 2064392 | tf_op jit(solution)/shard_map/ppermute | solution.py:356
  69.3 7.8 %collective-permute-start.1 = (bf16[16,192,128]{2,1,0:T(8,128)(2,1)S(1)}, bf16[16,192,128]{2,1,0:T(8,128)(2,1)S(1)}, u32[]{:S(2)}, u32[]{:S(2)}) collective-permute-start(bf16[16,192,128]{2,1,0:T(8,128)(2,1)S(1)} %all_to_all.17.own_ref.refs_3_), channel_id=1, source_target_pairs={{0,16},{16,0},{32,48},{48,32},{64,80},{80,64},{96,112},{112,96},{1... | collective-permute-start | bytes 2359304 | tf_op jit(solution)/shard_map/ppermute | solution.py:362

commit v5 on v4

--- a/solution.py
+++ b/solution.py
@@ -179,22 +179,31 @@
     return jnp.broadcast_to(x, (8, LANES))
 
 
+def added(terms):
+    while len(terms) > 1:
+        terms = [terms[i] + terms[i + 1] for i in range(0, len(terms), 2)]
+    return terms[0]
+
+
 def inverse_factor(gram):
     width = 8
     groups = LANES // width
     w = [gram[width * g : width * (g + 1), :] for g in range(groups)]
     row_of = lax.broadcasted_iota(jnp.int32, (width, LANES), 0)
     lane_of = lax.broadcasted_iota(jnp.int32, (width, LANES), 1)
+    pivots = [spread(w[0], lane=i) for i in range(width)]
     for g in range(groups):
         first = width * g
-        column = {h: [spread(w[h], lane=first + i) for i in range(width)] for h in range(g, groups)}
+        more = g + 1 < groups
+        column = {h: [spread(w[h], lane=first + i) for i in range(width)] for h in range(g + 1, groups)}
+        ahead = [spread(w[g + 1], lane=first + width + n) for n in range(width)] if more else []
         inside = (lane_of >= first) & (lane_of < first + width)
         start = jnp.where(inside, jnp.where(lane_of - first == row_of, 1.0, 0.0), w[g])
         y = [spread(start, row=m) for m in range(width)]
-        d = [[spread(column[g][i], row=m) for i in range(m + 1)] for m in range(width)]
+        d = [[spread(pivots[i], row=m) for i in range(m + 1)] for m in range(width)]
         low = [[None] * width for _ in range(width)]
         root = [None] * width
-        lead = list(column[g + 1]) if g + 1 < groups else None
+        lead = list(column[g + 1]) if more else None
         for i in range(width):
             if i % 2 == 0:
                 first_root = lax.rsqrt(d[i][i])
@@ -210,7 +219,7 @@
             y[i] = y[i] * root[i]
             for m in range(i + 1, width):
                 y[m] = y[m] - low[m][i] * y[i]
-            if lead is not None:
+            if more:
                 lead[i] = lead[i] * root[i]
                 for m in range(i + 1, width):
                     lead[m] = lead[m] - low[m][i] * lead[i]
@@ -222,10 +231,10 @@
             z[m] = value * root[m]
         for h in range(g + 1, groups):
             left, right = (lead, y) if h == g + 1 else (column[h], z)
-            terms = [left[i] * right[i] for i in range(width)]
-            while len(terms) > 1:
-                terms = [terms[i] + terms[i + 1] for i in range(0, len(terms), 2)]
-            w[h] = jnp.where(inside, 0.0, w[h]) - terms[0]
+            w[h] = jnp.where(inside, 0.0, w[h]) - added([left[i] * right[i] for i in range(width)])
+        pivots = [
+            ahead[n] - added([lead[i] * spread(lead[i], row=n) for i in range(width)]) for n in range(len(ahead))
+        ]
         rows = y[0]
         for m in range(1, width):
             rows = jnp.where(row_of == m, y[m], rows)
@@ -233,9 +242,7 @@
     return jnp.concatenate(w, axis=0)
 
 
-def basis_kernel(own_ref, other_ref, out_ref):
-    half = out_ref.shape[1]
-
+def basis_kernel(core_ref, own_ref, other_ref, out_ref):
     def left_half(ref):
         parts = [parted(ref[piece, MAIN:, :].astype(F32)[8:, :]) for piece in range(CHIPS)]
         lower = [jnp.where(upper_rows(), parts[2 * k][1], parts[2 * k + 1][1]) for k in range(CHIPS // 2)]
@@ -246,23 +253,27 @@
             x, y, (dims, ((), ())), precision=lax.Precision.HIGHEST, preferred_element_type=F32
         )
 
-    halves = left_half(own_ref), left_half(other_ref)
-    squares = [jnp.sum(p * p, axis=0, keepdims=True) for p in halves]
-    scale = lax.rsqrt(squares[0] + squares[1])
-    halves = [p * scale for p in halves]
-    grams = [product(p, p, ((0,), (0,))) for p in halves]
-    inverse = inverse_factor(grams[0] + grams[1])
-    for at, p in enumerate(halves):
-        out_ref[at] = product(p, inverse, ((1,), (1,))).astype(BF16)
-
-
-def bases(own, other, half):
+    half = out_ref.shape[1]
+    own, other = left_half(own_ref), left_half(other_ref)
+    is_first = core_ref[0] == 0
+    p = jnp.concatenate([jnp.where(is_first, own, other), jnp.where(is_first, other, own)], axis=0)
+    p = p * lax.rsqrt(jnp.sum(p * p, axis=0, keepdims=True))
+    inverse = inverse_factor(product(p, p, ((0,), (0,))))
+    basis = product(p, inverse, ((1,), (1,))).astype(BF16)
+    out_ref[0] = basis[:half, :]
+    out_ref[1] = basis[half:, :]
+
+
+def bases(core, own, other, half):
+    vmem = pl.BlockSpec(memory_space=pltpu.VMEM)
     return pl.pallas_call(
         basis_kernel,
         out_shape=jax.ShapeDtypeStruct((2, half, LANES), BF16),
+        in_specs=[pl.BlockSpec(memory_space=pltpu.SMEM), vmem, vmem],
+        out_specs=vmem,
         compiler_params=params(),
         name="basis",
-    )(own, other)
+    )(core, own, other)
 
 
 def finish_kernel(
@@ -297,7 +308,7 @@
     def pair_of(read, pair):
         return jnp.concatenate([read(2 * pair), read(2 * pair + 1)], axis=1)
 
-    basis = (basis_ref[0], basis_ref[1])
+    basis = (basis_ref[core], basis_ref[1 - core])
     flipped = [b.astype(F32).T.astype(BF16) for b in basis]
     copies = []
     for pair in range(q_ref.shape[0] // (2 * LANES)):
@@ -309,16 +320,16 @@
         scaled = (terms[0] + terms[1]) * (1.0 / replicas)
         q_ref[columns, :] = scaled.T.astype(BF16)
         right = scaled.astype(BF16)
-        for which, ref, b in ((core, own_ref, basis[0]), (1 - core, other_ref, basis[1])):
+        for at, (which, ref, b) in enumerate(((core, own_ref, basis[0]), (1 - core, other_ref, basis[1]))):
             mine = pair_of(lambda slab: ref[slab * half : (slab + 1) * half, :], pair).astype(F32)
             rows = pl.ds(pl.multiple_of(which * half, half), half)
             error_ref[rows, columns] = (mine - jnp.dot(b, right, preferred_element_type=F32)).astype(BF16)
-        copies += [
-            pltpu.make_async_copy(q_ref.at[columns, :], q_out.at[columns, :], sems.at[0, pair]),
-            pltpu.make_async_copy(error_ref.at[:, columns], error_out.at[:, columns], sems.at[1, pair]),
-        ]
-        for copy in copies[-2:]:
-            copy.start()
+            copies.append(
+                pltpu.make_async_copy(error_ref.at[rows, columns], error_out.at[rows, columns], sems.at[at, pair])
+            )
+            copies[-1].start()
+        copies.append(pltpu.make_async_copy(q_ref.at[columns, :], q_out.at[columns, :], sems.at[2, pair]))
+        copies[-1].start()
     for copy in copies:
         copy.wait()
 
@@ -334,7 +345,7 @@
         scratch_shapes=[
             pltpu.VMEM((rows, cols), BF16),
             pltpu.VMEM((cols, LANES), BF16),
-            pltpu.SemaphoreType.DMA((2, cols // (2 * LANES))),
+            pltpu.SemaphoreType.DMA((3, cols // (2 * LANES))),
         ],
         compiler_params=params(),
         name="finish",
@@ -360,7 +371,7 @@
     left = lax.all_to_all(left, "tensor", 0, 0)
     gathered = across_chips(repack(left, total))
     gathered_other = lax.ppermute(gathered, "dp", twin)
-    basis = bases(gathered, gathered_other, half)
+    basis = bases(core, gathered, gathered_other, half)
     new_error, q_next = finish(core, own, other, gathered, gathered_other, basis, replicas)
     return (new_error[None], q_next)
 

time: 84.6 us -> 83.6 us (0.988)
  Pallas kernels: 11 us -> 9.99 us
    pallas_call x1, Pallas kernels: 4.6 us -> 3.53 us  [bases(): pl.pallas_call(basis_kernel, out_shape=jax.ShapeDtypeStruct((2, half, LAN...]
where the time goes in v5:
time: 83.6 us; the launch traced here: 83.3 us
  blocking collectives  56 us (67%)
  starting transfers between devices  14.7 us (18%)
  Pallas kernels  9.99 us (12%)
  waiting for transfers between devices  1.91 us (2%)
    all_to_all x2, blocking collectives, across_chips(): return lax.all_to_all(pieces, 'dp', 0, 0, axis_index_groups=same_core)  31.1 us
    all_to_all x1, blocking collectives, on_device(): left = lax.all_to_all(left, 'tensor', 0, 0)  25 us
    ppermute x1, starting transfers between devices, on_device(): got = lax.ppermute(other, 'dp', twin)  8.79 us
    ppermute x1, starting transfers between devices, on_device(): gathered_other = lax.ppermute(gathered, 'dp', twin)  5.88 us
    pallas_call x1, Pallas kernels, bases(): pl.pallas_call(basis_kernel, out_shape=jax.ShapeDtypeStruct((2, half, LAN...  3.53 us
    pallas_call x2, Pallas kernels, half_call(): pl.pallas_call(kernel, out_shape=(out, jax.ShapeDtypeStruct((half, LANES)...  3.17 us
    pallas_call x1, Pallas kernels, finish(): pl.pallas_call(lambda *refs: finish_kernel(replicas, *refs), out_shape=(j...  2.67 us
    ppermute x1, waiting for transfers between devices, on_device(): gathered_other = lax.ppermute(gathered, 'dp', twin)  1.89 us
  transfers between devices with their start and end apart: 2, of which 1 were waited for; matrix products, arithmetic and copies ran while one was open for 0% of the time, Pallas kernels for 2%

profile of v5, /device:TPU:1, one launch (start us, length us, event | category | flops | bytes accessed | tf_op | source)
XLA Modules:
  0.0 83.3 jit_solution(2130335030578224594)
XLA Ops:
  0.6 0.0 copy-start
  0.7 1.5 %sent.1.refs_2_ = bf16[2688,128]{1,0:T(8,128)(2,1)S(1)} custom-call(s32[1]{0:T(128)} %bitcast.core_ref.refs_0_, bf16[384,1792]{1,0:T(8,128)(2,1)} %bitcast.4, bf16[384,1792]{1,0:T(8,128)(2,1)} %bitcast.6), custom_call_target="tpu_custom_call" | custom-call | tf_op jit(solution)/shard_map/sent/pallas_call | solution.py:72
  2.1 8.8 %collective-permute-start = (bf16[2688,128]{1,0:T(8,128)(2,1)S(1)}, bf16[2688,128]{1,0:T(8,128)(2,1)S(1)}, u32[]{:S(2)}, u32[]{:S(2)}) collective-permute-start(bf16[2688,128]{1,0:T(8,128)(2,1)S(1)} %sent.1.refs_2_), channel_id=1, source_target_pairs={{0,16},{16,0},{32,48},{48,32},{64,80},{80,64},{96,112},{112,96},{1... | collective-permute-start | bytes 2064392 | tf_op jit(solution)/shard_map/ppermute | solution.py:367
  10.9 0.0 copy-done
  10.9 1.7 %kept.1 = (bf16[2688,128]{1,0:T(8,128)(2,1)S(1)}, f32[192,128]{1,0:T(8,128)S(1)}) custom-call(s32[1]{0:T(128)} %bitcast.core_ref.refs_0_, bf16[384,1792]{1,0:T(8,128)(2,1)} %bitcast.5, bf16[384,1792]{1,0:T(8,128)(2,1)} %bitcast.7, bf16[1792,128]{1,0:T(8,128)(2,1)S(1)} %copy-done), custom_call_target="tpu_custom_call" | custom-call | tf_op jit(solution)/shard_map/kept/pallas_call | solution.py:72
  12.6 0.0 collective-permute-done.got_ref
  12.7 0.4 pack.1
  13.1 16.7 %all_to_all.15.in_ref = bf16[16,192,128]{2,1,0:T(8,128)(2,1)S(1)} all-to-all(bf16[16,192,128]{2,1,0:T(8,128)(2,1)S(1)} %pack.1), channel_id=1, replica_groups={{0,32,64,96,128,160,192,224,256,288,320,352,384,416,448,480},{16,48,80,..., dimensions={0} | all-to-all | bytes 1572864 | tf_op jit(solution)/shard_map/all_to_all | solution.py:364
  29.8 0.1 sums.1
  29.9 25.0 %all_to_all.16.left_ref = bf16[16,24,128]{2,1,0:T(8,128)(2,1)S(1)} all-to-all(bf16[16,24,128]{2,1,0:T(8,128)(2,1)S(1)} %get-tuple-element.10), channel_id=1, replica_groups=mesh['dp'=32,'tensor'=16] {'tensor'}, dimensions={0} | all-to-all | bytes 196608 | tf_op jit(solution)/shard_map/all_to_all | solution.py:371
  54.9 0.1 repack.1
  55.0 14.4 %all_to_all.17.own_ref.refs_3_ = bf16[16,192,128]{2,1,0:T(8,128)(2,1)S(1)} all-to-all(bf16[16,192,128]{2,1,0:T(8,128)(2,1)S(1)} %repack.1), channel_id=1, replica_groups={{0,32,64,96,128,160,192,224,256,288,320,352,384,416,448,480},{16,48,80,..., dimensions={0} | all-to-all | bytes 1572864 | tf_op jit(solution)/shard_map/all_to_all | solution.py:364
  69.3 5.9 %collective-permute-start.1 = (bf16[16,192,128]{2,1,0:T(8,128)(2,1)S(1)}, bf16[16,192,128]{2,1,0:T(8,128)(2,1)S(1)}, u32[]{:S(2)}, u32[]{:S(2)}) collective-permute-start(bf16[16,192,128]{2,1,0:T(8,128)(2,1)S(1)} %all_to_all.17.own_ref.refs_3_), channel_id=1, source_target_pairs={{0,16},{16,0},{32,48},{48,32},{64,80},{80,64},{96,112},{112,96},{1... | collective-permute-start | bytes 2359304 | tf_op jit(solution)/shard_map/ppermute | solution.py:373
  75.2 1.9 %collective-permute-done.1.other_ref.refs_4_ = bf16[16,192,128]{2,1,0:T(8,128)(2,1)S(1)} collective-permute-done((bf16[16,192,128]{2,1,0:T(8,128)(2,1)S(1)}, bf16[16,192,128]{2,1,0:T(8,128)(2,1)S(1)}, u32[]{:S(2)}, u32[]{:S(2)}) %collective-permute-start.1) | collective-permute-done | bytes 786464 | tf_op jit(solution)/shard_map/ppermute | solution.py:373
  77.1 3.5 %basis.1.refs_5_ = bf16[2,192,128]{2,1,0:T(8,128)(2,1)S(1)} custom-call(s32[1]{0:T(128)} %bitcast.core_ref.refs_0_, bf16[16,192,128]{2,1,0:T(8,128)(2,1)S(1)} %all_to_all.17.own_ref.refs_3_, bf16[16,192,128]{2,1,0:T(8,128)(2,1)S(1)} %collective-permute-done.1.other_ref.refs_4_), custom_call_target="tpu_custom_call" | custom-call | tf_op jit(solution)/shard_map/basis/pallas_call | solution.py:269
  80.6 2.7 %finish.1 = (bf16[384,1792]{1,0:T(8,128)(2,1)}, bf16[1792,128]{1,0:T(8,128)(2,1)}) custom-call(s32[1]{0:T(128)} %bitcast.core_ref.refs_0_, bf16[2688,128]{1,0:T(8,128)(2,1)S(1)} %get-tuple-element.8.own_ref.refs_1_, bf16[2688,128]{1,0:T(8,128)(2,1)S(1)} %sent.1.refs_2_, bf16[16,192,128]{2,1,0:T(8,128)(2,1)S(1)} %all_to_all.17.own_ref.refs_3_, ...), custom_call_target="tpu_custom_call" | custom-call | tf_op jit(solution)/shard_map/finish/pallas_call | solution.py:340
Async XLA Ops:
  0.6 10.3 %copy-start = (bf16[1792,128]{1,0:T(8,128)(2,1)S(1)}, bf16[1792,128]{1,0:T(8,128)(2,1)}, u32[]{:S(2)}) copy-start(bf16[1792,128]{1,0:T(8,128)(2,1)} %q_ref.3) | copy-start | bytes 1376260
  2.1 10.5 %collective-permute-start = (bf16[2688,128]{1,0:T(8,128)(2,1)S(1)}, bf16[2688,128]{1,0:T(8,128)(2,1)S(1)}, u32[]{:S(2)}, u32[]{:S(2)}) collective-permute-start(bf16[2688,128]{1,0:T(8,128)(2,1)S(1)} %sent.1.refs_2_), channel_id=1, source_target_pairs={{0,16},{16,0},{32,48},{48,32},{64,80},{80,64},{96,112},{112,96},{1... | collective-permute-start | bytes 2064392 | tf_op jit(solution)/shard_map/ppermute | solution.py:367
  69.3 7.8 %collective-permute-start.1 = (bf16[16,192,128]{2,1,0:T(8,128)(2,1)S(1)}, bf16[16,192,128]{2,1,0:T(8,128)(2,1)S(1)}, u32[]{:S(2)}, u32[]{:S(2)}) collective-permute-start(bf16[16,192,128]{2,1,0:T(8,128)(2,1)S(1)} %all_to_all.17.own_ref.refs_3_), channel_id=1, source_target_pairs={{0,16},{16,0},{32,48},{48,32},{64,80},{80,64},{96,112},{112,96},{1... | collective-permute-start | bytes 2359304 | tf_op jit(solution)/shard_map/ppermute | solution.py:373

commit v6 on v5

--- a/solution.py
+++ b/solution.py
@@ -311,25 +311,34 @@
     basis = (basis_ref[core], basis_ref[1 - core])
     flipped = [b.astype(F32).T.astype(BF16) for b in basis]
     copies = []
-    for pair in range(q_ref.shape[0] // (2 * LANES)):
-        columns = slice(2 * pair * LANES, 2 * (pair + 1) * LANES)
+    pairs = q_ref.shape[0] // (2 * LANES)
+
+    def right_of(pair):
         terms = [
             jnp.dot(flat, pair_of(lambda slab: slab_of(ref, slab), pair), preferred_element_type=F32)
             for flat, ref in zip(flipped, (own_sum_ref, other_sum_ref))
         ]
-        scaled = (terms[0] + terms[1]) * (1.0 / replicas)
-        q_ref[columns, :] = scaled.T.astype(BF16)
+        return (terms[0] + terms[1]) * (1.0 / replicas)
+
+    def send(source, target, sem):
+        copies.append(pltpu.make_async_copy(source, target, sem))
+        copies[-1].start()
+
+    ready = [right_of(pair) for pair in range(2)]
+    for pair in range(pairs):
+        columns = slice(2 * pair * LANES, 2 * (pair + 1) * LANES)
+        scaled = ready.pop(0)
         right = scaled.astype(BF16)
-        for at, (which, ref, b) in enumerate(((core, own_ref, basis[0]), (1 - core, other_ref, basis[1]))):
+        if pair + 2 < pairs:
+            ready.append(right_of(pair + 2))
+        products = [jnp.dot(b, right, preferred_element_type=F32) for b in basis]
+        for at, (which, ref) in enumerate(((core, own_ref), (1 - core, other_ref))):
             mine = pair_of(lambda slab: ref[slab * half : (slab + 1) * half, :], pair).astype(F32)
             rows = pl.ds(pl.multiple_of(which * half, half), half)
-            error_ref[rows, columns] = (mine - jnp.dot(b, right, preferred_element_type=F32)).astype(BF16)
-            copies.append(
-                pltpu.make_async_copy(error_ref.at[rows, columns], error_out.at[rows, columns], sems.at[at, pair])
-            )
-            copies[-1].start()
-        copies.append(pltpu.make_async_copy(q_ref.at[columns, :], q_out.at[columns, :], sems.at[2, pair]))
-        copies[-1].start()
+            error_ref[rows, columns] = (mine - products[at]).astype(BF16)
+            send(error_ref.at[rows, columns], error_out.at[rows, columns], sems.at[at, pair])
+        q_ref[columns, :] = scaled.T.astype(BF16)
+        send(q_ref.at[columns, :], q_out.at[columns, :], sems.at[2, pair])
     for copy in copies:
         copy.wait()
 

time: 83.6 us -> 82.8 us (level)
  no operation moved by 1% of the time
where the time goes in v6:
time: 82.8 us; the launch traced here: 82.5 us
  blocking collectives  56 us (68%)
  starting transfers between devices  14.7 us (18%)
  Pallas kernels  9.2 us (11%)
  waiting for transfers between devices  1.91 us (2%)
    all_to_all x2, blocking collectives, across_chips(): return lax.all_to_all(pieces, 'dp', 0, 0, axis_index_groups=same_core)  31.1 us
    all_to_all x1, blocking collectives, on_device(): left = lax.all_to_all(left, 'tensor', 0, 0)  25 us
    ppermute x1, starting transfers between devices, on_device(): got = lax.ppermute(other, 'dp', twin)  8.79 us
    ppermute x1, starting transfers between devices, on_device(): gathered_other = lax.ppermute(gathered, 'dp', twin)  5.88 us
    pallas_call x1, Pallas kernels, bases(): pl.pallas_call(basis_kernel, out_shape=jax.ShapeDtypeStruct((2, half, LAN...  3.53 us
    pallas_call x2, Pallas kernels, half_call(): pl.pallas_call(kernel, out_shape=(out, jax.ShapeDtypeStruct((half, LANES)...  3.17 us
    ppermute x1, waiting for transfers between devices, on_device(): gathered_other = lax.ppermute(gathered, 'dp', twin)  1.89 us
    pallas_call x1, Pallas kernels, finish(): pl.pallas_call(lambda *refs: finish_kernel(replicas, *refs), out_shape=(j...  1.88 us
  transfers between devices with their start and end apart: 2, of which 1 were waited for; matrix products, arithmetic and copies ran while one was open for 0% of the time, Pallas kernels for 2%

profile of v6, /device:TPU:1, one launch (start us, length us, event | category | flops | bytes accessed | tf_op | source)
XLA Modules:
  0.0 82.5 jit_solution(17563733433116368666)
XLA Ops:
  0.6 0.0 copy-start
  0.7 1.5 %sent.1.refs_2_ = bf16[2688,128]{1,0:T(8,128)(2,1)S(1)} custom-call(s32[1]{0:T(128)} %bitcast.core_ref.refs_0_, bf16[384,1792]{1,0:T(8,128)(2,1)} %bitcast.4, bf16[384,1792]{1,0:T(8,128)(2,1)} %bitcast.6), custom_call_target="tpu_custom_call" | custom-call | tf_op jit(solution)/shard_map/sent/pallas_call | solution.py:72
  2.1 8.8 %collective-permute-start = (bf16[2688,128]{1,0:T(8,128)(2,1)S(1)}, bf16[2688,128]{1,0:T(8,128)(2,1)S(1)}, u32[]{:S(2)}, u32[]{:S(2)}) collective-permute-start(bf16[2688,128]{1,0:T(8,128)(2,1)S(1)} %sent.1.refs_2_), channel_id=1, source_target_pairs={{0,16},{16,0},{32,48},{48,32},{64,80},{80,64},{96,112},{112,96},{1... | collective-permute-start | bytes 2064392 | tf_op jit(solution)/shard_map/ppermute | solution.py:376
  10.9 0.0 copy-done
  10.9 1.7 %kept.1 = (bf16[2688,128]{1,0:T(8,128)(2,1)S(1)}, f32[192,128]{1,0:T(8,128)S(1)}) custom-call(s32[1]{0:T(128)} %bitcast.core_ref.refs_0_, bf16[384,1792]{1,0:T(8,128)(2,1)} %bitcast.5, bf16[384,1792]{1,0:T(8,128)(2,1)} %bitcast.7, bf16[1792,128]{1,0:T(8,128)(2,1)S(1)} %copy-done), custom_call_target="tpu_custom_call" | custom-call | tf_op jit(solution)/shard_map/kept/pallas_call | solution.py:72
  12.6 0.0 collective-permute-done.got_ref
  12.7 0.4 pack.1
  13.1 16.7 %all_to_all.15.in_ref = bf16[16,192,128]{2,1,0:T(8,128)(2,1)S(1)} all-to-all(bf16[16,192,128]{2,1,0:T(8,128)(2,1)S(1)} %pack.1), channel_id=1, replica_groups={{0,32,64,96,128,160,192,224,256,288,320,352,384,416,448,480},{16,48,80,..., dimensions={0} | all-to-all | bytes 1572864 | tf_op jit(solution)/shard_map/all_to_all | solution.py:373
  29.8 0.1 sums.1
  29.9 25.0 %all_to_all.16.left_ref = bf16[16,24,128]{2,1,0:T(8,128)(2,1)S(1)} all-to-all(bf16[16,24,128]{2,1,0:T(8,128)(2,1)S(1)} %get-tuple-element.10), channel_id=1, replica_groups=mesh['dp'=32,'tensor'=16] {'tensor'}, dimensions={0} | all-to-all | bytes 196608 | tf_op jit(solution)/shard_map/all_to_all | solution.py:380
  54.9 0.1 repack.1
  55.0 14.4 %all_to_all.17.own_ref.refs_3_ = bf16[16,192,128]{2,1,0:T(8,128)(2,1)S(1)} all-to-all(bf16[16,192,128]{2,1,0:T(8,128)(2,1)S(1)} %repack.1), channel_id=1, replica_groups={{0,32,64,96,128,160,192,224,256,288,320,352,384,416,448,480},{16,48,80,..., dimensions={0} | all-to-all | bytes 1572864 | tf_op jit(solution)/shard_map/all_to_all | solution.py:373
  69.3 5.9 %collective-permute-start.1 = (bf16[16,192,128]{2,1,0:T(8,128)(2,1)S(1)}, bf16[16,192,128]{2,1,0:T(8,128)(2,1)S(1)}, u32[]{:S(2)}, u32[]{:S(2)}) collective-permute-start(bf16[16,192,128]{2,1,0:T(8,128)(2,1)S(1)} %all_to_all.17.own_ref.refs_3_), channel_id=1, source_target_pairs={{0,16},{16,0},{32,48},{48,32},{64,80},{80,64},{96,112},{112,96},{1... | collective-permute-start | bytes 2359304 | tf_op jit(solution)/shard_map/ppermute | solution.py:382
  75.2 1.9 %collective-permute-done.1.other_ref.refs_4_ = bf16[16,192,128]{2,1,0:T(8,128)(2,1)S(1)} collective-permute-done((bf16[16,192,128]{2,1,0:T(8,128)(2,1)S(1)}, bf16[16,192,128]{2,1,0:T(8,128)(2,1)S(1)}, u32[]{:S(2)}, u32[]{:S(2)}) %collective-permute-start.1) | collective-permute-done | bytes 786464 | tf_op jit(solution)/shard_map/ppermute | solution.py:382
  77.1 3.5 %basis.1.refs_5_ = bf16[2,192,128]{2,1,0:T(8,128)(2,1)S(1)} custom-call(s32[1]{0:T(128)} %bitcast.core_ref.refs_0_, bf16[16,192,128]{2,1,0:T(8,128)(2,1)S(1)} %all_to_all.17.own_ref.refs_3_, bf16[16,192,128]{2,1,0:T(8,128)(2,1)S(1)} %collective-permute-done.1.other_ref.refs_4_), custom_call_target="tpu_custom_call" | custom-call | tf_op jit(solution)/shard_map/basis/pallas_call | solution.py:269
  80.6 1.9 %finish.1 = (bf16[384,1792]{1,0:T(8,128)(2,1)}, bf16[1792,128]{1,0:T(8,128)(2,1)}) custom-call(s32[1]{0:T(128)} %bitcast.core_ref.refs_0_, bf16[2688,128]{1,0:T(8,128)(2,1)S(1)} %get-tuple-element.8.own_ref.refs_1_, bf16[2688,128]{1,0:T(8,128)(2,1)S(1)} %sent.1.refs_2_, bf16[16,192,128]{2,1,0:T(8,128)(2,1)S(1)} %all_to_all.17.own_ref.refs_3_, ...), custom_call_target="tpu_custom_call" | custom-call | tf_op jit(solution)/shard_map/finish/pallas_call | solution.py:349
Async XLA Ops:
  0.6 10.3 %copy-start = (bf16[1792,128]{1,0:T(8,128)(2,1)S(1)}, bf16[1792,128]{1,0:T(8,128)(2,1)}, u32[]{:S(2)}) copy-start(bf16[1792,128]{1,0:T(8,128)(2,1)} %q_ref.3) | copy-start | bytes 1376260
  2.1 10.5 %collective-permute-start = (bf16[2688,128]{1,0:T(8,128)(2,1)S(1)}, bf16[2688,128]{1,0:T(8,128)(2,1)S(1)}, u32[]{:S(2)}, u32[]{:S(2)}) collective-permute-start(bf16[2688,128]{1,0:T(8,128)(2,1)S(1)} %sent.1.refs_2_), channel_id=1, source_target_pairs={{0,16},{16,0},{32,48},{48,32},{64,80},{80,64},{96,112},{112,96},{1... | collective-permute-start | bytes 2064392 | tf_op jit(solution)/shard_map/ppermute | solution.py:376
  69.3 7.8 %collective-permute-start.1 = (bf16[16,192,128]{2,1,0:T(8,128)(2,1)S(1)}, bf16[16,192,128]{2,1,0:T(8,128)(2,1)S(1)}, u32[]{:S(2)}, u32[]{:S(2)}) collective-permute-start(bf16[16,192,128]{2,1,0:T(8,128)(2,1)S(1)} %all_to_all.17.own_ref.refs_3_), channel_id=1, source_target_pairs={{0,16},{16,0},{32,48},{48,32},{64,80},{80,64},{96,112},{112,96},{1... | collective-permute-start | bytes 2359304 | tf_op jit(solution)/shard_map/ppermute | solution.py:382

commit v7 on v6

--- a/solution.py
+++ b/solution.py
@@ -242,38 +242,32 @@
     return jnp.concatenate(w, axis=0)
 
 
-def basis_kernel(core_ref, own_ref, other_ref, out_ref):
-    def left_half(ref):
-        parts = [parted(ref[piece, MAIN:, :].astype(F32)[8:, :]) for piece in range(CHIPS)]
-        lower = [jnp.where(upper_rows(), parts[2 * k][1], parts[2 * k + 1][1]) for k in range(CHIPS // 2)]
-        return jnp.concatenate([eight for eight, _ in parts] + lower, axis=0)
-
-    def product(x, y, dims):
-        return lax.dot_general(
-            x, y, (dims, ((), ())), precision=lax.Precision.HIGHEST, preferred_element_type=F32
-        )
-
-    half = out_ref.shape[1]
-    own, other = left_half(own_ref), left_half(other_ref)
-    is_first = core_ref[0] == 0
-    p = jnp.concatenate([jnp.where(is_first, own, other), jnp.where(is_first, other, own)], axis=0)
+def left_half(ref):
+    parts = [parted(ref[piece, MAIN:, :].astype(F32)[8:, :]) for piece in range(CHIPS)]
+    lower = [jnp.where(upper_rows(), parts[2 * k][1], parts[2 * k + 1][1]) for k in range(CHIPS // 2)]
+    return jnp.concatenate([eight for eight, _ in parts] + lower, axis=0)
+
+
+def own_rows_kernel(in_ref, out_ref):
+    out_ref[...] = left_half(in_ref)
+
+
+def own_rows(pieces, half):
+    return pl.pallas_call(
+        own_rows_kernel,
+        out_shape=jax.ShapeDtypeStruct((half, LANES), F32),
+        compiler_params=params(),
+        name="own_rows",
+    )(pieces)
+
+
+def flipped_basis(p):
+    def product(x, y):
+        return jnp.dot(x, y, precision=lax.Precision.HIGHEST, preferred_element_type=F32)
+
     p = p * lax.rsqrt(jnp.sum(p * p, axis=0, keepdims=True))
-    inverse = inverse_factor(product(p, p, ((0,), (0,))))
-    basis = product(p, inverse, ((1,), (1,))).astype(BF16)
-    out_ref[0] = basis[:half, :]
-    out_ref[1] = basis[half:, :]
-
-
-def bases(core, own, other, half):
-    vmem = pl.BlockSpec(memory_space=pltpu.VMEM)
-    return pl.pallas_call(
-        basis_kernel,
-        out_shape=jax.ShapeDtypeStruct((2, half, LANES), BF16),
-        in_specs=[pl.BlockSpec(memory_space=pltpu.SMEM), vmem, vmem],
-        out_specs=vmem,
-        compiler_params=params(),
-        name="basis",
-    )(core, own, other)
+    flipped = p.T
+    return product(inverse_factor(product(flipped, p)), flipped)
 
 
 def finish_kernel(
@@ -283,15 +277,16 @@
     other_ref,
     own_sum_ref,
     other_sum_ref,
-    basis_ref,
+    p_ref,
     error_out,
     q_out,
     error_ref,
     q_ref,
+    basis_ref,
     sems,
 ):
     core = core_ref[0]
-    half = basis_ref.shape[1]
+    half = p_ref.shape[0]
 
     def slab_of(ref, slab):
         at, end, parts = slab * half, (slab + 1) * half, []
@@ -308,17 +303,23 @@
     def pair_of(read, pair):
         return jnp.concatenate([read(2 * pair), read(2 * pair + 1)], axis=1)
 
+    is_first = core == 0
+
+    def in_order(own, other):
+        return jnp.concatenate([jnp.where(is_first, own, other), jnp.where(is_first, other, own)], axis=0)
+
+    flipped = flipped_basis(in_order(p_ref[...], left_half(other_sum_ref)))
+    rows_of_basis = flipped.T.astype(BF16)
+    flipped = flipped.astype(BF16)
+    basis_ref[0] = rows_of_basis[:half, :]
+    basis_ref[1] = rows_of_basis[half:, :]
     basis = (basis_ref[core], basis_ref[1 - core])
-    flipped = [b.astype(F32).T.astype(BF16) for b in basis]
     copies = []
     pairs = q_ref.shape[0] // (2 * LANES)
 
     def right_of(pair):
-        terms = [
-            jnp.dot(flat, pair_of(lambda slab: slab_of(ref, slab), pair), preferred_element_type=F32)
-            for flat, ref in zip(flipped, (own_sum_ref, other_sum_ref))
-        ]
-        return (terms[0] + terms[1]) * (1.0 / replicas)
+        sums = in_order(*(pair_of(lambda slab: slab_of(ref, slab), pair) for ref in (own_sum_ref, other_sum_ref)))
+        return jnp.dot(flipped, sums, preferred_element_type=F32) * (1.0 / replicas)
 
     def send(source, target, sem):
         copies.append(pltpu.make_async_copy(source, target, sem))
@@ -343,8 +344,8 @@
         copy.wait()
 
 
-def finish(core, own, other, own_sum, other_sum, basis, replicas):
-    rows, cols = 2 * basis.shape[1], own.shape[0] // basis.shape[1] * LANES
+def finish(core, own, other, own_sum, other_sum, p_own, cols, replicas):
+    rows = 2 * p_own.shape[0]
     vmem = pl.BlockSpec(memory_space=pltpu.VMEM)
     return pl.pallas_call(
         lambda *refs: finish_kernel(replicas, *refs),
@@ -354,11 +355,12 @@
         scratch_shapes=[
             pltpu.VMEM((rows, cols), BF16),
             pltpu.VMEM((cols, LANES), BF16),
+            pltpu.VMEM((2, rows // 2, LANES), BF16),
             pltpu.SemaphoreType.DMA((3, cols // (2 * LANES))),
         ],
         compiler_params=params(),
         name="finish",
-    )(core, own, other, own_sum, other_sum, basis)
+    )(core, own, other, own_sum, other_sum, p_own)
 
 
 def on_device(gradient, error, q_prev):
@@ -380,8 +382,8 @@
     left = lax.all_to_all(left, "tensor", 0, 0)
     gathered = across_chips(repack(left, total))
     gathered_other = lax.ppermute(gathered, "dp", twin)
-    basis = bases(core, gathered, gathered_other, half)
-    new_error, q_next = finish(core, own, other, gathered, gathered_other, basis, replicas)
+    p_own = own_rows(gathered, half)
+    new_error, q_next = finish(core, own, other, gathered, gathered_other, p_own, cols, replicas)
     return (new_error[None], q_next)
 
 

time: 82.8 us -> 82.7 us (level)
    pallas_call x1, Pallas kernels: 3.53 us -> 0.02 us  [own_rows(): pl.pallas_call(own_rows_kernel, out_shape=jax.ShapeDtypeStruct((half, LAN...]
    pallas_call x1, Pallas kernels: 1.88 us -> 5.27 us  [finish(): pl.pallas_call(lambda *refs: finish_kernel(replicas, *refs), out_shape=(j...]
where the time goes in v7:
time: 82.7 us; the launch traced here: 82.4 us
  blocking collectives  56 us (68%)
  starting transfers between devices  14.7 us (18%)
  Pallas kernels  9.09 us (11%)
  waiting for transfers between devices  1.89 us (2%)
    all_to_all x2, blocking collectives, across_chips(): return lax.all_to_all(pieces, 'dp', 0, 0, axis_index_groups=same_core)  31.1 us
    all_to_all x1, blocking collectives, on_device(): left = lax.all_to_all(left, 'tensor', 0, 0)  25 us
    ppermute x1, starting transfers between devices, on_device(): got = lax.ppermute(other, 'dp', twin)  8.79 us
    ppermute x1, starting transfers between devices, on_device(): gathered_other = lax.ppermute(gathered, 'dp', twin)  5.88 us
    pallas_call x1, Pallas kernels, finish(): pl.pallas_call(lambda *refs: finish_kernel(replicas, *refs), out_shape=(j...  5.27 us
    pallas_call x2, Pallas kernels, half_call(): pl.pallas_call(kernel, out_shape=(out, jax.ShapeDtypeStruct((half, LANES)...  3.17 us
    ppermute x1, waiting for transfers between devices, on_device(): gathered_other = lax.ppermute(gathered, 'dp', twin)  1.86 us
  transfers between devices with their start and end apart: 2, of which 1 were waited for; matrix products, arithmetic and copies ran while one was open for 0% of the time, Pallas kernels for 2%

profile of v7, /device:TPU:1, one launch (start us, length us, event | category | flops | bytes accessed | tf_op | source)
XLA Modules:
  0.0 82.4 jit_solution(16224386097938523796)
XLA Ops:
  0.6 0.0 copy-start
  0.7 1.5 %sent.1.refs_2_ = bf16[2688,128]{1,0:T(8,128)(2,1)S(1)} custom-call(s32[1]{0:T(128)} %bitcast.core_ref.refs_0_, bf16[384,1792]{1,0:T(8,128)(2,1)} %bitcast.4, bf16[384,1792]{1,0:T(8,128)(2,1)} %bitcast.6), custom_call_target="tpu_custom_call" | custom-call | tf_op jit(solution)/shard_map/sent/pallas_call | solution.py:72
  2.1 8.8 %collective-permute-start = (bf16[2688,128]{1,0:T(8,128)(2,1)S(1)}, bf16[2688,128]{1,0:T(8,128)(2,1)S(1)}, u32[]{:S(2)}, u32[]{:S(2)}) collective-permute-start(bf16[2688,128]{1,0:T(8,128)(2,1)S(1)} %sent.1.refs_2_), channel_id=1, source_target_pairs={{0,16},{16,0},{32,48},{48,32},{64,80},{80,64},{96,112},{112,96},{1... | collective-permute-start | bytes 2064392 | tf_op jit(solution)/shard_map/ppermute | solution.py:378
  10.9 0.0 copy-done
  10.9 1.7 %kept.1 = (bf16[2688,128]{1,0:T(8,128)(2,1)S(1)}, f32[192,128]{1,0:T(8,128)S(1)}) custom-call(s32[1]{0:T(128)} %bitcast.core_ref.refs_0_, bf16[384,1792]{1,0:T(8,128)(2,1)} %bitcast.5, bf16[384,1792]{1,0:T(8,128)(2,1)} %bitcast.7, bf16[1792,128]{1,0:T(8,128)(2,1)S(1)} %copy-done), custom_call_target="tpu_custom_call" | custom-call | tf_op jit(solution)/shard_map/kept/pallas_call | solution.py:72
  12.6 0.0 collective-permute-done.got_ref
  12.7 0.4 pack.1
  13.1 16.7 %all_to_all.15.in_ref = bf16[16,192,128]{2,1,0:T(8,128)(2,1)S(1)} all-to-all(bf16[16,192,128]{2,1,0:T(8,128)(2,1)S(1)} %pack.1), channel_id=1, replica_groups={{0,32,64,96,128,160,192,224,256,288,320,352,384,416,448,480},{16,48,80,..., dimensions={0} | all-to-all | bytes 1572864 | tf_op jit(solution)/shard_map/all_to_all | solution.py:375
  29.8 0.1 sums.1
  29.9 25.0 %all_to_all.16.left_ref = bf16[16,24,128]{2,1,0:T(8,128)(2,1)S(1)} all-to-all(bf16[16,24,128]{2,1,0:T(8,128)(2,1)S(1)} %get-tuple-element.10), channel_id=1, replica_groups=mesh['dp'=32,'tensor'=16] {'tensor'}, dimensions={0} | all-to-all | bytes 196608 | tf_op jit(solution)/shard_map/all_to_all | solution.py:382
  54.9 0.1 repack.1
  55.0 14.4 %all_to_all.17.in_ref.refs_3_ = bf16[16,192,128]{2,1,0:T(8,128)(2,1)S(1)} all-to-all(bf16[16,192,128]{2,1,0:T(8,128)(2,1)S(1)} %repack.1), channel_id=1, replica_groups={{0,32,64,96,128,160,192,224,256,288,320,352,384,416,448,480},{16,48,80,..., dimensions={0} | all-to-all | bytes 1572864 | tf_op jit(solution)/shard_map/all_to_all | solution.py:375
  69.3 5.9 %collective-permute-start.1 = (bf16[16,192,128]{2,1,0:T(8,128)(2,1)S(1)}, bf16[16,192,128]{2,1,0:T(8,128)(2,1)S(1)}, u32[]{:S(2)}, u32[]{:S(2)}) collective-permute-start(bf16[16,192,128]{2,1,0:T(8,128)(2,1)S(1)} %all_to_all.17.in_ref.refs_3_), channel_id=1, source_target_pairs={{0,16},{16,0},{32,48},{48,32},{64,80},{80,64},{96,112},{112,96},{1... | collective-permute-start | bytes 2359304 | tf_op jit(solution)/shard_map/ppermute | solution.py:384
  75.2 1.9 %collective-permute-done.1.refs_4_ = bf16[16,192,128]{2,1,0:T(8,128)(2,1)S(1)} collective-permute-done((bf16[16,192,128]{2,1,0:T(8,128)(2,1)S(1)}, bf16[16,192,128]{2,1,0:T(8,128)(2,1)S(1)}, u32[]{:S(2)}, u32[]{:S(2)}) %collective-permute-start.1) | collective-permute-done | bytes 786464 | tf_op jit(solution)/shard_map/ppermute | solution.py:384
  77.1 5.3 %finish.1 = (bf16[384,1792]{1,0:T(8,128)(2,1)}, bf16[1792,128]{1,0:T(8,128)(2,1)}) custom-call(s32[1]{0:T(128)} %bitcast.core_ref.refs_0_, bf16[2688,128]{1,0:T(8,128)(2,1)S(1)} %get-tuple-element.8.own_ref.refs_1_, bf16[2688,128]{1,0:T(8,128)(2,1)S(1)} %sent.1.refs_2_, bf16[16,192,128]{2,1,0:T(8,128)(2,1)S(1)} %all_to_all.17.in_ref.refs_3_, ...), custom_call_target="tpu_custom_call" | custom-call | tf_op jit(solution)/shard_map/finish/pallas_call | solution.py:350
  (1 shorter events, 0.0 us)
Async XLA Ops:
  0.6 10.3 %copy-start = (bf16[1792,128]{1,0:T(8,128)(2,1)S(1)}, bf16[1792,128]{1,0:T(8,128)(2,1)}, u32[]{:S(2)}) copy-start(bf16[1792,128]{1,0:T(8,128)(2,1)} %q_ref.3) | copy-start | bytes 1376260
  2.1 10.5 %collective-permute-start = (bf16[2688,128]{1,0:T(8,128)(2,1)S(1)}, bf16[2688,128]{1,0:T(8,128)(2,1)S(1)}, u32[]{:S(2)}, u32[]{:S(2)}) collective-permute-start(bf16[2688,128]{1,0:T(8,128)(2,1)S(1)} %sent.1.refs_2_), channel_id=1, source_target_pairs={{0,16},{16,0},{32,48},{48,32},{64,80},{80,64},{96,112},{112,96},{1... | collective-permute-start | bytes 2064392 | tf_op jit(solution)/shard_map/ppermute | solution.py:378
  69.3 7.8 %collective-permute-start.1 = (bf16[16,192,128]{2,1,0:T(8,128)(2,1)S(1)}, bf16[16,192,128]{2,1,0:T(8,128)(2,1)S(1)}, u32[]{:S(2)}, u32[]{:S(2)}) collective-permute-start(bf16[16,192,128]{2,1,0:T(8,128)(2,1)S(1)} %all_to_all.17.in_ref.refs_3_), channel_id=1, source_target_pairs={{0,16},{16,0},{32,48},{48,32},{64,80},{80,64},{96,112},{112,96},{1... | collective-permute-start | bytes 2359304 | tf_op jit(solution)/shard_map/ppermute | solution.py:384

commit v8 on v6

--- a/solution.py
+++ b/solution.py
@@ -10,6 +10,10 @@
 CHIPS = 16
 MAIN = 160
 MIXED = 32
+ORDERS = (
+    [10, 11, 8, 13, 14, 0, 9, 7, 6, 15, 1, 3, 2, 12, 4, 5],
+    [5, 6, 10, 11, 8, 4, 7, 0, 1, 15, 2, 3, 13, 14, 9, 12],
+)
 VMEM_LIMIT = 48 * 1024 * 1024
 SENT_LIMIT = 52 * 1024 * 1024
 KEPT_LIMIT = 52 * 1024 * 1024
@@ -367,7 +371,7 @@
     half = rows // 2
     core = (lax.axis_index("dp") % 2).astype(jnp.int32).reshape(1)
     twin = [(i, i ^ 1) for i in range(replicas)]
-    same_core = [[2 * chip + c for chip in range(CHIPS)] for c in range(2)]
+    same_core = [[2 * chip + c for chip in ORDERS[c]] for c in range(2)]
 
     def across_chips(pieces):
         return lax.all_to_all(pieces, "dp", 0, 0, axis_index_groups=same_core)

time: 82.8 us -> 81.6 us (0.986)
  starting transfers between devices: 14.7 us -> 12.6 us
  blocking collectives: 56 us -> 56.9 us
    all_to_all x2, blocking collectives: 31.1 us -> 33.9 us  [across_chips(): return lax.all_to_all(pieces, 'dp', 0, 0, axis_index_groups=same_core)]
    ppermute x1, starting transfers between devices: 5.88 us -> 3.78 us  [on_device(): gathered_other = lax.ppermute(gathered, 'dp', twin)]
    all_to_all x1, blocking collectives: 25 us -> 23.1 us  [on_device(): left = lax.all_to_all(left, 'tensor', 0, 0)]
where the time goes in v8:
time: 81.6 us; the launch traced here: 81.3 us
  blocking collectives  56.9 us (70%)
  starting transfers between devices  12.6 us (15%)
  Pallas kernels  9.21 us (11%)
  waiting for transfers between devices  1.91 us (2%)
    all_to_all x2, blocking collectives, across_chips(): return lax.all_to_all(pieces, 'dp', 0, 0, axis_index_groups=same_core)  33.9 us
    all_to_all x1, blocking collectives, on_device(): left = lax.all_to_all(left, 'tensor', 0, 0)  23.1 us
    ppermute x1, starting transfers between devices, on_device(): got = lax.ppermute(other, 'dp', twin)  8.79 us
    ppermute x1, starting transfers between devices, on_device(): gathered_other = lax.ppermute(gathered, 'dp', twin)  3.78 us
    pallas_call x1, Pallas kernels, bases(): pl.pallas_call(basis_kernel, out_shape=jax.ShapeDtypeStruct((2, half, LAN...  3.53 us
    pallas_call x2, Pallas kernels, half_call(): pl.pallas_call(kernel, out_shape=(out, jax.ShapeDtypeStruct((half, LANES)...  3.17 us
    ppermute x1, waiting for transfers between devices, on_device(): gathered_other = lax.ppermute(gathered, 'dp', twin)  1.89 us
    pallas_call x1, Pallas kernels, finish(): pl.pallas_call(lambda *refs: finish_kernel(replicas, *refs), out_shape=(j...  1.88 us
  transfers between devices with their start and end apart: 2, of which 1 were waited for; matrix products, arithmetic and copies ran while one was open for 0% of the time, Pallas kernels for 2%

profile of v8, /device:TPU:1, one launch (start us, length us, event | category | flops | bytes accessed | tf_op | source)
XLA Modules:
  0.0 81.3 jit_solution(8894100643747085755)
XLA Ops:
  0.6 0.0 copy-start
  0.7 1.5 %sent.1.refs_2_ = bf16[2688,128]{1,0:T(8,128)(2,1)S(1)} custom-call(s32[1]{0:T(128)} %bitcast.core_ref.refs_0_, bf16[384,1792]{1,0:T(8,128)(2,1)} %bitcast.4, bf16[384,1792]{1,0:T(8,128)(2,1)} %bitcast.6), custom_call_target="tpu_custom_call" | custom-call | tf_op jit(solution)/shard_map/sent/pallas_call | solution.py:76
  2.1 8.8 %collective-permute-start = (bf16[2688,128]{1,0:T(8,128)(2,1)S(1)}, bf16[2688,128]{1,0:T(8,128)(2,1)S(1)}, u32[]{:S(2)}, u32[]{:S(2)}) collective-permute-start(bf16[2688,128]{1,0:T(8,128)(2,1)S(1)} %sent.1.refs_2_), channel_id=1, source_target_pairs={{0,16},{16,0},{32,48},{48,32},{64,80},{80,64},{96,112},{112,96},{1... | collective-permute-start | bytes 2064392 | tf_op jit(solution)/shard_map/ppermute | solution.py:380
  10.9 0.0 copy-done
  10.9 1.7 %kept.1 = (bf16[2688,128]{1,0:T(8,128)(2,1)S(1)}, f32[192,128]{1,0:T(8,128)S(1)}) custom-call(s32[1]{0:T(128)} %bitcast.core_ref.refs_0_, bf16[384,1792]{1,0:T(8,128)(2,1)} %bitcast.5, bf16[384,1792]{1,0:T(8,128)(2,1)} %bitcast.7, bf16[1792,128]{1,0:T(8,128)(2,1)S(1)} %copy-done), custom_call_target="tpu_custom_call" | custom-call | tf_op jit(solution)/shard_map/kept/pallas_call | solution.py:76
  12.6 0.0 collective-permute-done.got_ref
  12.7 0.4 pack.1
  13.1 16.9 %all_to_all.15.in_ref = bf16[16,192,128]{2,1,0:T(8,128)(2,1)S(1)} all-to-all(bf16[16,192,128]{2,1,0:T(8,128)(2,1)S(1)} %pack.1), channel_id=1, replica_groups={{320,352,256,416,448,0,288,224,192,480,32,96,64,384,128,160},{176,208,3..., dimensions={0} | all-to-all | bytes 1572864 | tf_op jit(solution)/shard_map/all_to_all | solution.py:377
  30.0 0.1 sums.1
  30.1 23.1 %all_to_all.16.left_ref = bf16[16,24,128]{2,1,0:T(8,128)(2,1)S(1)} all-to-all(bf16[16,24,128]{2,1,0:T(8,128)(2,1)S(1)} %get-tuple-element.10), channel_id=1, replica_groups=mesh['dp'=32,'tensor'=16] {'tensor'}, dimensions={0} | all-to-all | bytes 196608 | tf_op jit(solution)/shard_map/all_to_all | solution.py:384
  53.2 0.1 repack.1
  53.3 16.9 %all_to_all.17.own_ref.refs_3_ = bf16[16,192,128]{2,1,0:T(8,128)(2,1)S(1)} all-to-all(bf16[16,192,128]{2,1,0:T(8,128)(2,1)S(1)} %repack.1), channel_id=1, replica_groups={{320,352,256,416,448,0,288,224,192,480,32,96,64,384,128,160},{176,208,3..., dimensions={0} | all-to-all | bytes 1572864 | tf_op jit(solution)/shard_map/all_to_all | solution.py:377
  70.2 3.8 %collective-permute-start.1 = (bf16[16,192,128]{2,1,0:T(8,128)(2,1)S(1)}, bf16[16,192,128]{2,1,0:T(8,128)(2,1)S(1)}, u32[]{:S(2)}, u32[]{:S(2)}) collective-permute-start(bf16[16,192,128]{2,1,0:T(8,128)(2,1)S(1)} %all_to_all.17.own_ref.refs_3_), channel_id=1, source_target_pairs={{0,16},{16,0},{32,48},{48,32},{64,80},{80,64},{96,112},{112,96},{1... | collective-permute-start | bytes 2359304 | tf_op jit(solution)/shard_map/ppermute | solution.py:386
  74.0 1.9 %collective-permute-done.1.other_ref.refs_4_ = bf16[16,192,128]{2,1,0:T(8,128)(2,1)S(1)} collective-permute-done((bf16[16,192,128]{2,1,0:T(8,128)(2,1)S(1)}, bf16[16,192,128]{2,1,0:T(8,128)(2,1)S(1)}, u32[]{:S(2)}, u32[]{:S(2)}) %collective-permute-start.1) | collective-permute-done | bytes 786464 | tf_op jit(solution)/shard_map/ppermute | solution.py:386
  75.9 3.5 %basis.1.refs_5_ = bf16[2,192,128]{2,1,0:T(8,128)(2,1)S(1)} custom-call(s32[1]{0:T(128)} %bitcast.core_ref.refs_0_, bf16[16,192,128]{2,1,0:T(8,128)(2,1)S(1)} %all_to_all.17.own_ref.refs_3_, bf16[16,192,128]{2,1,0:T(8,128)(2,1)S(1)} %collective-permute-done.1.other_ref.refs_4_), custom_call_target="tpu_custom_call" | custom-call | tf_op jit(solution)/shard_map/basis/pallas_call | solution.py:273
  79.4 1.9 %finish.1 = (bf16[384,1792]{1,0:T(8,128)(2,1)}, bf16[1792,128]{1,0:T(8,128)(2,1)}) custom-call(s32[1]{0:T(128)} %bitcast.core_ref.refs_0_, bf16[2688,128]{1,0:T(8,128)(2,1)S(1)} %get-tuple-element.8.own_ref.refs_1_, bf16[2688,128]{1,0:T(8,128)(2,1)S(1)} %sent.1.refs_2_, bf16[16,192,128]{2,1,0:T(8,128)(2,1)S(1)} %all_to_all.17.own_ref.refs_3_, ...), custom_call_target="tpu_custom_call" | custom-call | tf_op jit(solution)/shard_map/finish/pallas_call | solution.py:353
Async XLA Ops:
  0.6 10.3 %copy-start = (bf16[1792,128]{1,0:T(8,128)(2,1)S(1)}, bf16[1792,128]{1,0:T(8,128)(2,1)}, u32[]{:S(2)}) copy-start(bf16[1792,128]{1,0:T(8,128)(2,1)} %q_ref.3) | copy-start | bytes 1376260
  2.1 10.5 %collective-permute-start = (bf16[2688,128]{1,0:T(8,128)(2,1)S(1)}, bf16[2688,128]{1,0:T(8,128)(2,1)S(1)}, u32[]{:S(2)}, u32[]{:S(2)}) collective-permute-start(bf16[2688,128]{1,0:T(8,128)(2,1)S(1)} %sent.1.refs_2_), channel_id=1, source_target_pairs={{0,16},{16,0},{32,48},{48,32},{64,80},{80,64},{96,112},{112,96},{1... | collective-permute-start | bytes 2064392 | tf_op jit(solution)/shard_map/ppermute | solution.py:380
  70.2 5.7 %collective-permute-start.1 = (bf16[16,192,128]{2,1,0:T(8,128)(2,1)S(1)}, bf16[16,192,128]{2,1,0:T(8,128)(2,1)S(1)}, u32[]{:S(2)}, u32[]{:S(2)}) collective-permute-start(bf16[16,192,128]{2,1,0:T(8,128)(2,1)S(1)} %all_to_all.17.own_ref.refs_3_), channel_id=1, source_target_pairs={{0,16},{16,0},{32,48},{48,32},{64,80},{80,64},{96,112},{112,96},{1... | collective-permute-start | bytes 2359304 | tf_op jit(solution)/shard_map/ppermute | solution.py:386

commit v9 on v7

--- a/solution.py
+++ b/solution.py
@@ -10,6 +10,10 @@
 CHIPS = 16
 MAIN = 160
 MIXED = 32
+ORDERS = (
+    [10, 11, 8, 13, 14, 0, 9, 7, 6, 15, 1, 3, 2, 12, 4, 5],
+    [5, 6, 10, 11, 8, 4, 7, 0, 1, 15, 2, 3, 13, 14, 9, 12],
+)
 VMEM_LIMIT = 48 * 1024 * 1024
 SENT_LIMIT = 52 * 1024 * 1024
 KEPT_LIMIT = 52 * 1024 * 1024
@@ -248,19 +252,6 @@
     return jnp.concatenate([eight for eight, _ in parts] + lower, axis=0)
 
 
-def own_rows_kernel(in_ref, out_ref):
-    out_ref[...] = left_half(in_ref)
-
-
-def own_rows(pieces, half):
-    return pl.pallas_call(
-        own_rows_kernel,
-        out_shape=jax.ShapeDtypeStruct((half, LANES), F32),
-        compiler_params=params(),
-        name="own_rows",
-    )(pieces)
-
-
 def flipped_basis(p):
     def product(x, y):
         return jnp.dot(x, y, precision=lax.Precision.HIGHEST, preferred_element_type=F32)
@@ -277,7 +268,6 @@
     other_ref,
     own_sum_ref,
     other_sum_ref,
-    p_ref,
     error_out,
     q_out,
     error_ref,
@@ -286,7 +276,7 @@
     sems,
 ):
     core = core_ref[0]
-    half = p_ref.shape[0]
+    half = basis_ref.shape[1]
 
     def slab_of(ref, slab):
         at, end, parts = slab * half, (slab + 1) * half, []
@@ -308,7 +298,7 @@
     def in_order(own, other):
         return jnp.concatenate([jnp.where(is_first, own, other), jnp.where(is_first, other, own)], axis=0)
 
-    flipped = flipped_basis(in_order(p_ref[...], left_half(other_sum_ref)))
+    flipped = flipped_basis(in_order(left_half(own_sum_ref), left_half(other_sum_ref)))
     rows_of_basis = flipped.T.astype(BF16)
     flipped = flipped.astype(BF16)
     basis_ref[0] = rows_of_basis[:half, :]
@@ -344,13 +334,12 @@
         copy.wait()
 
 
-def finish(core, own, other, own_sum, other_sum, p_own, cols, replicas):
-    rows = 2 * p_own.shape[0]
+def finish(core, own, other, own_sum, other_sum, rows, cols, replicas):
     vmem = pl.BlockSpec(memory_space=pltpu.VMEM)
     return pl.pallas_call(
         lambda *refs: finish_kernel(replicas, *refs),
         out_shape=(jax.ShapeDtypeStruct((rows, cols), BF16), jax.ShapeDtypeStruct((cols, LANES), BF16)),
-        in_specs=[pl.BlockSpec(memory_space=pltpu.SMEM)] + [vmem] * 5,
+        in_specs=[pl.BlockSpec(memory_space=pltpu.SMEM)] + [vmem] * 4,
         out_specs=(pl.BlockSpec(memory_space=pl.ANY),) * 2,
         scratch_shapes=[
             pltpu.VMEM((rows, cols), BF16),
@@ -360,7 +349,7 @@
         ],
         compiler_params=params(),
         name="finish",
-    )(core, own, other, own_sum, other_sum, p_own)
+    )(core, own, other, own_sum, other_sum)
 
 
 def on_device(gradient, error, q_prev):
@@ -369,7 +358,7 @@
     half = rows // 2
     core = (lax.axis_index("dp") % 2).astype(jnp.int32).reshape(1)
     twin = [(i, i ^ 1) for i in range(replicas)]
-    same_core = [[2 * chip + c for chip in range(CHIPS)] for c in range(2)]
+    same_core = [[2 * chip + c for chip in ORDERS[c]] for c in range(2)]
 
     def across_chips(pieces):
         return lax.all_to_all(pieces, "dp", 0, 0, axis_index_groups=same_core)
@@ -382,8 +371,7 @@
     left = lax.all_to_all(left, "tensor", 0, 0)
     gathered = across_chips(repack(left, total))
     gathered_other = lax.ppermute(gathered, "dp", twin)
-    p_own = own_rows(gathered, half)
-    new_error, q_next = finish(core, own, other, gathered, gathered_other, p_own, cols, replicas)
+    new_error, q_next = finish(core, own, other, gathered, gathered_other, rows, cols, replicas)
     return (new_error[None], q_next)
 
 

time: 82.7 us -> 81.5 us (0.985)
  starting transfers between devices: 14.7 us -> 12.6 us
  blocking collectives: 56 us -> 56.9 us
    all_to_all x2, blocking collectives: 31.1 us -> 33.9 us  [across_chips(): return lax.all_to_all(pieces, 'dp', 0, 0, axis_index_groups=same_core)]
    ppermute x1, starting transfers between devices: 5.88 us -> 3.78 us  [on_device(): gathered_other = lax.ppermute(gathered, 'dp', twin)]
    all_to_all x1, blocking collectives: 25 us -> 23.1 us  [on_device(): left = lax.all_to_all(left, 'tensor', 0, 0)]
where the time goes in v9:
time: 81.5 us; the launch traced here: 81.2 us
  blocking collectives  56.9 us (70%)
  starting transfers between devices  12.6 us (15%)
  Pallas kernels  9.09 us (11%)
  waiting for transfers between devices  1.91 us (2%)
    all_to_all x2, blocking collectives, across_chips(): return lax.all_to_all(pieces, 'dp', 0, 0, axis_index_groups=same_core)  33.9 us
    all_to_all x1, blocking collectives, on_device(): left = lax.all_to_all(left, 'tensor', 0, 0)  23.1 us
    ppermute x1, starting transfers between devices, on_device(): got = lax.ppermute(other, 'dp', twin)  8.79 us
    pallas_call x1, Pallas kernels, finish(): pl.pallas_call(lambda *refs: finish_kernel(replicas, *refs), out_shape=(j...  5.29 us
    ppermute x1, starting transfers between devices, on_device(): gathered_other = lax.ppermute(gathered, 'dp', twin)  3.78 us
    pallas_call x2, Pallas kernels, half_call(): pl.pallas_call(kernel, out_shape=(out, jax.ShapeDtypeStruct((half, LANES)...  3.17 us
    ppermute x1, waiting for transfers between devices, on_device(): gathered_other = lax.ppermute(gathered, 'dp', twin)  1.89 us
  transfers between devices with their start and end apart: 2, of which 1 were waited for; matrix products, arithmetic and copies ran while one was open for 0% of the time, Pallas kernels for 2%

profile of v9, /device:TPU:1, one launch (start us, length us, event | category | flops | bytes accessed | tf_op | source)
XLA Modules:
  0.0 81.2 jit_solution(15970453307599264419)
XLA Ops:
  0.6 0.0 copy-start
  0.7 1.5 %sent.1.refs_2_ = bf16[2688,128]{1,0:T(8,128)(2,1)S(1)} custom-call(s32[1]{0:T(128)} %bitcast.core_ref.refs_0_, bf16[384,1792]{1,0:T(8,128)(2,1)} %bitcast.4, bf16[384,1792]{1,0:T(8,128)(2,1)} %bitcast.6), custom_call_target="tpu_custom_call" | custom-call | tf_op jit(solution)/shard_map/sent/pallas_call | solution.py:76
  2.1 8.8 %collective-permute-start = (bf16[2688,128]{1,0:T(8,128)(2,1)S(1)}, bf16[2688,128]{1,0:T(8,128)(2,1)S(1)}, u32[]{:S(2)}, u32[]{:S(2)}) collective-permute-start(bf16[2688,128]{1,0:T(8,128)(2,1)S(1)} %sent.1.refs_2_), channel_id=1, source_target_pairs={{0,16},{16,0},{32,48},{48,32},{64,80},{80,64},{96,112},{112,96},{1... | collective-permute-start | bytes 2064392 | tf_op jit(solution)/shard_map/ppermute | solution.py:367
  10.9 0.0 copy-done
  10.9 1.7 %kept.1 = (bf16[2688,128]{1,0:T(8,128)(2,1)S(1)}, f32[192,128]{1,0:T(8,128)S(1)}) custom-call(s32[1]{0:T(128)} %bitcast.core_ref.refs_0_, bf16[384,1792]{1,0:T(8,128)(2,1)} %bitcast.5, bf16[384,1792]{1,0:T(8,128)(2,1)} %bitcast.7, bf16[1792,128]{1,0:T(8,128)(2,1)S(1)} %copy-done), custom_call_target="tpu_custom_call" | custom-call | tf_op jit(solution)/shard_map/kept/pallas_call | solution.py:76
  12.6 0.0 collective-permute-done.got_ref
  12.7 0.4 pack.1
  13.1 16.9 %all_to_all.15.in_ref = bf16[16,192,128]{2,1,0:T(8,128)(2,1)S(1)} all-to-all(bf16[16,192,128]{2,1,0:T(8,128)(2,1)S(1)} %pack.1), channel_id=1, replica_groups={{320,352,256,416,448,0,288,224,192,480,32,96,64,384,128,160},{176,208,3..., dimensions={0} | all-to-all | bytes 1572864 | tf_op jit(solution)/shard_map/all_to_all | solution.py:364
  30.0 0.1 sums.1
  30.1 23.1 %all_to_all.16.left_ref = bf16[16,24,128]{2,1,0:T(8,128)(2,1)S(1)} all-to-all(bf16[16,24,128]{2,1,0:T(8,128)(2,1)S(1)} %get-tuple-element.10), channel_id=1, replica_groups=mesh['dp'=32,'tensor'=16] {'tensor'}, dimensions={0} | all-to-all | bytes 196608 | tf_op jit(solution)/shard_map/all_to_all | solution.py:371
  53.2 0.1 repack.1
  53.3 16.9 %all_to_all.17.refs_3_ = bf16[16,192,128]{2,1,0:T(8,128)(2,1)S(1)} all-to-all(bf16[16,192,128]{2,1,0:T(8,128)(2,1)S(1)} %repack.1), channel_id=1, replica_groups={{320,352,256,416,448,0,288,224,192,480,32,96,64,384,128,160},{176,208,3..., dimensions={0} | all-to-all | bytes 1572864 | tf_op jit(solution)/shard_map/all_to_all | solution.py:364
  70.2 3.8 %collective-permute-start.1 = (bf16[16,192,128]{2,1,0:T(8,128)(2,1)S(1)}, bf16[16,192,128]{2,1,0:T(8,128)(2,1)S(1)}, u32[]{:S(2)}, u32[]{:S(2)}) collective-permute-start(bf16[16,192,128]{2,1,0:T(8,128)(2,1)S(1)} %all_to_all.17.refs_3_), channel_id=1, source_target_pairs={{0,16},{16,0},{32,48},{48,32},{64,80},{80,64},{96,112},{112,96},{1... | collective-permute-start | bytes 2359304 | tf_op jit(solution)/shard_map/ppermute | solution.py:373
  74.0 1.9 %collective-permute-done.1.refs_4_ = bf16[16,192,128]{2,1,0:T(8,128)(2,1)S(1)} collective-permute-done((bf16[16,192,128]{2,1,0:T(8,128)(2,1)S(1)}, bf16[16,192,128]{2,1,0:T(8,128)(2,1)S(1)}, u32[]{:S(2)}, u32[]{:S(2)}) %collective-permute-start.1) | collective-permute-done | bytes 786464 | tf_op jit(solution)/shard_map/ppermute | solution.py:373
  75.9 5.3 %finish.1 = (bf16[384,1792]{1,0:T(8,128)(2,1)}, bf16[1792,128]{1,0:T(8,128)(2,1)}) custom-call(s32[1]{0:T(128)} %bitcast.core_ref.refs_0_, bf16[2688,128]{1,0:T(8,128)(2,1)S(1)} %get-tuple-element.8.own_ref.refs_1_, bf16[2688,128]{1,0:T(8,128)(2,1)S(1)} %sent.1.refs_2_, bf16[16,192,128]{2,1,0:T(8,128)(2,1)S(1)} %all_to_all.17.refs_3_, ...), custom_call_target="tpu_custom_call" | custom-call | tf_op jit(solution)/shard_map/finish/pallas_call | solution.py:339
Async XLA Ops:
  0.6 10.3 %copy-start = (bf16[1792,128]{1,0:T(8,128)(2,1)S(1)}, bf16[1792,128]{1,0:T(8,128)(2,1)}, u32[]{:S(2)}) copy-start(bf16[1792,128]{1,0:T(8,128)(2,1)} %q_ref.3) | copy-start | bytes 1376260
  2.1 10.5 %collective-permute-start = (bf16[2688,128]{1,0:T(8,128)(2,1)S(1)}, bf16[2688,128]{1,0:T(8,128)(2,1)S(1)}, u32[]{:S(2)}, u32[]{:S(2)}) collective-permute-start(bf16[2688,128]{1,0:T(8,128)(2,1)S(1)} %sent.1.refs_2_), channel_id=1, source_target_pairs={{0,16},{16,0},{32,48},{48,32},{64,80},{80,64},{96,112},{112,96},{1... | collective-permute-start | bytes 2064392 | tf_op jit(solution)/shard_map/ppermute | solution.py:367
  70.2 5.7 %collective-permute-start.1 = (bf16[16,192,128]{2,1,0:T(8,128)(2,1)S(1)}, bf16[16,192,128]{2,1,0:T(8,128)(2,1)S(1)}, u32[]{:S(2)}, u32[]{:S(2)}) collective-permute-start(bf16[16,192,128]{2,1,0:T(8,128)(2,1)S(1)} %all_to_all.17.refs_3_), channel_id=1, source_target_pairs={{0,16},{16,0},{32,48},{48,32},{64,80},{80,64},{96,112},{112,96},{1... | collective-permute-start | bytes 2359304 | tf_op jit(solution)/shard_map/ppermute | solution.py:373
